TPU v7x, 32 devices: a whole 2x2x4 slice. The times are simulated.
32 devices in a mesh: groups: 1, ep: 32 (over z, y, x, core).
Axes of the slice: x: 2, y: 2, z: 4, core: 2. Of those that a mesh axis runs over, the one named last changes fastest.
Arguments:
- kv_cache: bfloat16 [256, 32, 512], P(('groups', 'ep')), may hold values from -4.5 to 4.5
- cache_length: int32 [256], P(('groups', 'ep')), may hold values from 2 to 32, as said below
- dest_device: int32 [256], P(('groups', 'ep')), may hold values from 0 to 31, as said below
- dest_slot: int32 [256], P(('groups', 'ep')), may hold values from 0 to 7, as said below
- query_rows: bfloat16 [256, 4096], P(('groups', 'ep')), may hold values from -4.5 to 4.5
- new_kv: bfloat16 [256, 512], P(('groups', 'ep')), may hold values from -4.5 to 4.5
- resid_rows: bfloat16 [256, 4096], P(('groups', 'ep')), may hold values from -3 to 3
- norm_gain: bfloat16 [4096], replicated, may hold values from 0.099609375 to 1.8984375
- route_ids: int32 [256, 8], P(('groups', 'ep')), may hold values from 0 to 15, all different within a row; in each aligned block of 8 rows (0 to 7, 8 to 15, ...) at most 8 rows name the same one
- route_weight: bfloat16 [256, 8], P(('groups', 'ep')), may hold values from 0.049804688 to 0.3984375
- w_gate: bfloat16 [32, 4096, 384], P('ep'), may hold values from -0.09375 to 0.09375
- w_up: bfloat16 [32, 4096, 384], P('ep'), may hold values from -0.09375 to 0.09375
- w_down: bfloat16 [32, 384, 4096], P('ep'), may hold values from -0.21875 to 0.21875
Outputs:
- moved_cache: bfloat16 [256, 32, 512], P(('groups', 'ep'))
- context: bfloat16 [256, 4096], P(('groups', 'ep'))
- moe_out: bfloat16 [256, 4096], P(('groups', 'ep'))
Inputs may be any that keep to these rules, and one draw needn't show every extreme that they name: `dest_device`: device d hands exactly 2 of its requests to each of the devices d, d + 1, ..., d + 3 along ep (indices modulo the number of devices), so every device receives exactly 8 requests. `dest_slot`: the requests that arrive at one device take distinct slots. `cache_length`: every device holds a request of length exactly 32. `route_ids`: the 8 experts of a row differ; among the rows of one device no expert is named by more than 8 rows.
All inputs are finite; a program needn't handle non-finite values.
Results may differ from a plain program's by a relative error of at most 0.014.
Values may be sent and summed in bfloat16 or wider, within the bound.
A program may use at most 64 MiB of HBM per device.

v0:
```python
import math

import jax
import jax.numpy as jnp
from jax import lax
from jax.sharding import PartitionSpec as P

HEAD_DIM = 128
Q_HEADS = 32
KV_HEADS = 2
TOPK = 8
SPAN = 4
LEN = 32


def from_behind(array, axis, by):
    peers = lax.axis_size(axis)
    return lax.ppermute(array, axis, [(i, (i + by) % peers) for i in range(peers)])


def attend(query_rows, new_kv, kv_cache, cache_length):
    row_count = query_rows.shape[0]
    group_size = Q_HEADS // KV_HEADS
    score_scale = 1.0 / math.sqrt(HEAD_DIM)
    queries = query_rows.reshape(row_count, KV_HEADS, group_size, HEAD_DIM)
    stored = kv_cache.reshape(row_count, LEN, 2, KV_HEADS, HEAD_DIM)
    fresh = new_kv.reshape(row_count, 2, KV_HEADS, HEAD_DIM)
    scores = (
        jnp.einsum("rgjd,rtgd->rgjt", queries, stored[:, :, 0], preferred_element_type=jnp.float32)
        * score_scale
    )
    own_score = (
        jnp.einsum("rgjd,rgd->rgj", queries, fresh[:, 0], preferred_element_type=jnp.float32)
        * score_scale
    )
    in_range = (jnp.arange(LEN, dtype=jnp.int32)[None, :] < cache_length[:, None])[:, None, None, :]
    masked = jnp.where(in_range, scores, -jnp.inf)
    peak = jnp.maximum(jnp.max(masked, axis=-1), own_score)
    weights = jnp.where(in_range, jnp.exp(scores - peak[..., None]), 0.0)
    own_weight = jnp.exp(own_score - peak)
    denominator = jnp.sum(weights, axis=-1) + own_weight
    probs = (weights / denominator[..., None]).astype(jnp.bfloat16)
    own_prob = (own_weight / denominator).astype(jnp.bfloat16)
    context = jnp.einsum(
        "rgjt,rtgd->rgjd", probs, stored[:, :, 1], preferred_element_type=jnp.float32
    )
    context = (
        context
        + own_prob.astype(jnp.float32)[..., None] * fresh[:, 1].astype(jnp.float32)[:, :, None, :]
    )
    return context.reshape(row_count, Q_HEADS * HEAD_DIM).astype(jnp.bfloat16)


def expert_half(row_block, gate_matrix, up_matrix, down_matrix):
    gate_part = jnp.dot(row_block, gate_matrix, preferred_element_type=jnp.float32)
    up_part = jnp.dot(row_block, up_matrix, preferred_element_type=jnp.float32)
    hidden = (jax.nn.silu(gate_part) * up_part).astype(jnp.bfloat16)
    return jnp.dot(hidden, down_matrix, preferred_element_type=jnp.float32).astype(jnp.bfloat16)


def order_matrix(dest_device, device_count, owned_count, group_rows):
    offset = (dest_device - lax.axis_index("ep")) % device_count
    onehot = (offset[:, None] == jnp.arange(SPAN, dtype=jnp.int32)[None, :]).astype(jnp.int32)
    rank = jnp.sum((jnp.cumsum(onehot, axis=0) - onehot) * onehot, axis=1)
    position = offset * group_rows + rank
    return jnp.arange(owned_count, dtype=jnp.int32)[:, None] == position[None, :]


def apply_rows(selector, values):
    return jnp.dot(selector, values, preferred_element_type=jnp.float32).astype(jnp.bfloat16)


def shards(
    kv_cache,
    cache_length,
    dest_device,
    dest_slot,
    query_rows,
    new_kv,
    resid_rows,
    norm_gain,
    route_ids,
    route_weight,
    w_gate,
    w_up,
    w_down,
):
    device_count = lax.axis_size("ep")
    owned_count = kv_cache.shape[0]
    group_rows = owned_count // SPAN
    sender = order_matrix(dest_device, device_count, owned_count, group_rows)
    sender_int = sender.astype(jnp.int32)
    sender_bf = sender.astype(jnp.bfloat16)
    ordered = apply_rows(sender_bf, kv_cache.reshape(owned_count, -1)).reshape(SPAN, group_rows, -1)
    slot_meta = (jnp.sum(sender_int * (dest_slot + 1)[None, :], axis=1) - 1).reshape(
        SPAN, group_rows
    )
    length_meta = jnp.sum(sender_int * cache_length[None, :], axis=1).reshape(SPAN, group_rows)
    slot_range = jnp.arange(owned_count, dtype=jnp.int32)[:, None]
    cache_pieces = [ordered[0]]
    slot_pieces = [slot_meta[0]]
    length_pieces = [length_meta[0]]
    for offset in range(1, SPAN):
        got_cache, got_slot, got_length = from_behind(
            (ordered[offset], slot_meta[offset], length_meta[offset]), "ep", offset
        )
        cache_pieces.append(got_cache)
        slot_pieces.append(got_slot)
        length_pieces.append(got_length)
    incoming = jnp.concatenate(cache_pieces, axis=0)
    arrived_slot = jnp.concatenate(slot_pieces, axis=0)
    arrived_length = jnp.concatenate(length_pieces, axis=0)
    chooser = arrived_slot.reshape(1, owned_count) == slot_range
    moved_cache = apply_rows(chooser.astype(jnp.bfloat16), incoming).reshape(kv_cache.shape)
    moved_length = jnp.sum(
        chooser.astype(jnp.int32) * arrived_length.reshape(1, owned_count), axis=1
    )
    context = attend(query_rows, new_kv, moved_cache, moved_length)
    summed_state = resid_rows.astype(jnp.float32) + context.astype(jnp.float32)
    inverse = lax.rsqrt(jnp.mean(summed_state * summed_state, axis=1, keepdims=True) + 1e-06)
    normed = (summed_state * inverse * norm_gain.astype(jnp.float32)[None, :]).astype(jnp.bfloat16)
    width = normed.shape[1]
    experts = device_count // 2
    capacity = 2 * max(1, min(owned_count // 2, owned_count * TOPK // experts))
    flat_ids = route_ids.reshape(-1)
    onehot = (flat_ids[:, None] == jnp.arange(experts, dtype=jnp.int32)[None, :]).astype(jnp.int32)
    slot_index = jnp.sum((jnp.cumsum(onehot, axis=0) - onehot) * onehot, axis=1)
    position = flat_ids * capacity + slot_index
    hit_table = (
        position[:, None] == jnp.arange(experts * capacity, dtype=jnp.int32)[None, :]
    ).reshape(owned_count, TOPK, -1)
    gather_rows = jnp.sum(hit_table.astype(jnp.float32), axis=1).astype(jnp.bfloat16)
    blend_matrix = jnp.sum(
        jnp.where(hit_table, route_weight.astype(jnp.float32)[:, :, None], 0.0), axis=1
    ).astype(jnp.bfloat16)
    outgoing_rows = apply_rows(gather_rows.T, normed)
    doubled = jnp.broadcast_to(
        outgoing_rows.reshape(experts, 1, capacity, width), (experts, 2, capacity, width)
    )
    doubled = doubled.reshape(device_count, capacity, width)
    arrived = lax.all_to_all(doubled, "ep", split_axis=0, concat_axis=0, tiled=True)
    slot_count = arrived.shape[1]
    partial_value = expert_half(arrived.reshape(-1, width), w_gate[0], w_up[0], w_down[0])
    returned = lax.all_to_all(
        partial_value.reshape(device_count, slot_count, width),
        "ep",
        split_axis=0,
        concat_axis=0,
        tiled=True,
    )
    halves = returned.reshape(experts, 2, capacity, width).astype(jnp.float32)
    expert_out = (
        (halves[:, 0] + halves[:, 1]).astype(jnp.bfloat16).reshape(experts * capacity, width)
    )
    moe_out = apply_rows(blend_matrix, expert_out)
    return (moved_cache, context, moe_out)


def solution(mesh):
    placed = (
        P(("groups", "ep"), None, None),
        P(("groups", "ep")),
        P(("groups", "ep")),
        P(("groups", "ep")),
        P(("groups", "ep"), None),
        P(("groups", "ep"), None),
        P(("groups", "ep"), None),
        P(),
        P(("groups", "ep"), None),
        P(("groups", "ep"), None),
        P("ep", None, None),
        P("ep", None, None),
        P("ep", None, None),
    )
    return jax.shard_map(
        shards,
        mesh=mesh,
        in_specs=placed,
        out_specs=(
            P(("groups", "ep"), None, None),
            P(("groups", "ep"), None),
            P(("groups", "ep"), None),
        ),
        check_vma=False,
    )
```

profile of v0, /device:TPU:0, one launch (start us, length us, event | category | flops | bytes accessed | tf_op | source)
XLA Modules:
  0.0 148.9 jit_solution(1035291187944564236)
XLA Ops:
  0.7 0.8 and_select_fusion
  2.4 0.8 select_reduce_fusion.4
  3.3 2.4 %collective-permute-start.8 = (s32[2]{0:T(128)S(1)}, s32[2]{0:T(128)S(1)}, u32[]{:S(2)}, u32[]{:S(2)}) collective-permute-start(s32[2]{0:T(128)S(1)} %get-tuple-element.26), channel_id=1, source_target_pairs={{0,3},{1,4},{2,5},{3,6},{4,7},{5,8},{6,9},{7,10},{8,11},{9,12},{10... | collective-permute-start | bytes 32 | tf_op jit(solution)/shard_map/ppermute | solution.py:18
  5.6 1.5 %collective-permute-start.7 = (s32[2]{0:T(128)S(1)}, s32[2]{0:T(128)S(1)}, u32[]{:S(2)}, u32[]{:S(2)}) collective-permute-start(s32[2]{0:T(128)S(1)} %get-tuple-element.27), channel_id=1, source_target_pairs={{0,2},{1,3},{2,4},{3,5},{4,6},{5,7},{6,8},{7,9},{8,10},{9,11},{10,... | collective-permute-start | bytes 32 | tf_op jit(solution)/shard_map/ppermute | solution.py:18
  7.6 2.3 %collective-permute-start.2 = (s32[2]{0:T(128)S(1)}, s32[2]{0:T(128)S(1)}, u32[]{:S(2)}, u32[]{:S(2)}) collective-permute-start(s32[2]{0:T(128)S(1)} %get-tuple-element.30), channel_id=1, source_target_pairs={{0,3},{1,4},{2,5},{3,6},{4,7},{5,8},{6,9},{7,10},{8,11},{9,12},{10... | collective-permute-start | bytes 32 | tf_op jit(solution)/shard_map/ppermute | solution.py:18
  9.9 1.5 %collective-permute-start.1 = (s32[2]{0:T(128)S(1)}, s32[2]{0:T(128)S(1)}, u32[]{:S(2)}, u32[]{:S(2)}) collective-permute-start(s32[2]{0:T(128)S(1)} %get-tuple-element.31), channel_id=1, source_target_pairs={{0,2},{1,3},{2,4},{3,5},{4,6},{5,7},{6,8},{7,9},{8,10},{9,11},{10,... | collective-permute-start | bytes 32 | tf_op jit(solution)/shard_map/ppermute | solution.py:18
  11.4 0.8 eq.79
  15.3 0.7 multiply_add_fusion
  16.0 1.1 copy.31
  17.5 1.0 fusion.48
  19.2 2.7 %collective-permute-start.5 = (bf16[2,16384]{1,0:T(2,128)(2,1)S(1)}, bf16[2,16384]{1,0:T(2,128)(2,1)S(1)}, u32[]{:S(2)}, u32[]{:S(2)}) collective-permute-start(bf16[2,16384]{1,0:T(2,128)(2,1)S(1)} %get-tuple-element.18), channel_id=1, source_target_pairs={{0,3},{1,4},{2,5},{3,6},{4,7},{5,8},{6,9},{7,10},{8,11},{9,12},{10... | collective-permute-start | bytes 196616 | tf_op jit(solution)/shard_map/ppermute | solution.py:18
  21.9 1.5 %collective-permute-start.4 = (bf16[2,16384]{1,0:T(2,128)(2,1)S(1)}, bf16[2,16384]{1,0:T(2,128)(2,1)S(1)}, u32[]{:S(2)}, u32[]{:S(2)}) collective-permute-start(bf16[2,16384]{1,0:T(2,128)(2,1)S(1)} %get-tuple-element.19), channel_id=1, source_target_pairs={{0,2},{1,3},{2,4},{3,5},{4,6},{5,7},{6,8},{7,9},{8,10},{9,11},{10,... | collective-permute-start | bytes 196616 | tf_op jit(solution)/shard_map/ppermute | solution.py:18
  23.5 2.3 %collective-permute-done = s32[2]{0:T(128)S(1)} collective-permute-done((s32[2]{0:T(128)S(1)}, s32[2]{0:T(128)S(1)}, u32[]{:S(2)}, u32[]{:S(2)}) %collective-permute-start) | collective-permute-done | bytes 40 | tf_op jit(solution)/shard_map/ppermute | solution.py:18
  26.1 3.7 %collective-permute-done.4 = bf16[2,16384]{1,0:T(2,128)(2,1)S(1)} collective-permute-done((bf16[2,16384]{1,0:T(2,128)(2,1)S(1)}, bf16[2,16384]{1,0:T(2,128)(2,1)S(1)}, u32[]{:S(2)}, u32[]{:S(2)}) %collective-permute-start.4) | collective-permute-done | bytes 65568 | tf_op jit(solution)/shard_map/ppermute | solution.py:18
  29.8 1.0 collective-permute-done.3
  33.0 50.6 %all_to_all.10 = bf16[32,8,4096]{2,1,0:T(8,128)(2,1)S(1)} all-to-all(bf16[32,8,4096]{2,1,0:T(8,128)(2,1)S(1)} %bitcast.74), channel_id=1, replica_groups=mesh['groups'=1,'ep'=32] {'ep'}, dimensions={0} | all-to-all | bytes 4194304 | tf_op jit(solution)/shard_map/all_to_all | solution.py:141
  83.6 1.3 copy-done.1
  84.9 2.1 %fusion.5 = f32[256,384]{1,0:T(8,128)} fusion(bf16[1,4096,384]{2,1,0:T(8,128)(2,1)S(1)} %copy-done.6, bf16[32,8,4096]{2,1,0:T(8,128)(2,1)S(1)} %all_to_all.10), kind=kOutput, calls=%fused_computation.10 | convolution fusion | flops 805306368 | bytes 5636096 | tf_op jit(solution)/shard_map/dot_general | solution.py:55
  87.0 6.4 %fusion = bf16[32,8,4096]{2,1,0:T(8,128)(2,1)} fusion(bf16[1,384,4096]{2,1,0:T(8,128)(2,1)S(1)} %copy-done, bf16[1,4096,384]{2,1,0:T(8,128)(2,1)} %param.24, bf16[32,8,4096]{2,1,0:T(8,128)(2,1)} %copy-done.1, f32[256,384]{1,0:T(8,128)} %fusion.5), kind=kOutput, calls=%fused_computation.3 | convolution fusion | flops 1612251136 | bytes 10878976 | tf_op jit(solution)/shard_map/dot_general | solution.py:58
  93.3 3.7 %all-to-all-start.1 = ((bf16[32,8,4096]{2,1,0:T(8,128)(2,1)}), bf16[32,8,4096]{2,1,0:T(8,128)(2,1)}, u32[]{:S(2)}, u32[]{:S(2)}) async-start(bf16[32,8,4096]{2,1,0:T(8,128)(2,1)} %fusion), calls=%async_computation.1 | async-start | bytes 4194304 | tf_op jit(solution)/shard_map/all_to_all | solution.py:144
  97.0 0.8 copy.25
  97.8 48.1 %all-to-all-done.1 = bf16[32,8,4096]{2,1,0:T(8,128)(2,1)} async-done(((bf16[32,8,4096]{2,1,0:T(8,128)(2,1)}), bf16[32,8,4096]{2,1,0:T(8,128)(2,1)}, u32[]{:S(2)}, u32[]{:S(2)}) %all-to-all-start.1) | async-done | bytes 2097184 | tf_op jit(solution)/shard_map/all_to_all | solution.py:144
  145.9 2.1 %convert.2 = f32[16,2,8,4096]{3,2,1,0:T(8,128)S(1)} convert(bf16[16,2,8,4096]{3,2,1,0:T(8,128)(2,1)} %bitcast.20) | non-fusion elementwise | flops 1048576 | bytes 6291456 | tf_op jit(solution)/shard_map/convert_element_type | solution.py:151
  148.0 0.9 convolution_convert_fusion.4
  (57 shorter events, 8.2 us)
Async XLA Ops:
  0.6 86.3 %copy-start = (bf16[1,384,4096]{2,1,0:T(8,128)(2,1)S(1)}, bf16[1,384,4096]{2,1,0:T(8,128)(2,1)}, u32[]{:S(2)}) copy-start(bf16[1,384,4096]{2,1,0:T(8,128)(2,1)} %param.25) | copy-start | bytes 9437188
  0.6 30.6 %copy-start.7 = (bf16[8,4096]{1,0:T(8,128)(2,1)S(1)}, bf16[8,4096]{1,0:T(8,128)(2,1)}, u32[]{:S(2)}) copy-start(bf16[8,4096]{1,0:T(8,128)(2,1)} %param.17) | copy-start | bytes 196612
  0.7 31.4 %copy-start.2 = (bf16[8,4096]{1,0:T(8,128)(2,1)S(1)}, bf16[8,4096]{1,0:T(8,128)(2,1)}, u32[]{:S(2)}) copy-start(bf16[8,4096]{1,0:T(8,128)(2,1)} %param.19) | copy-start | bytes 196612
  3.3 16.0 %collective-permute-start.8 = (s32[2]{0:T(128)S(1)}, s32[2]{0:T(128)S(1)}, u32[]{:S(2)}, u32[]{:S(2)}) collective-permute-start(s32[2]{0:T(128)S(1)} %get-tuple-element.26), channel_id=1, source_target_pairs={{0,3},{1,4},{2,5},{3,6},{4,7},{5,8},{6,9},{7,10},{8,11},{9,12},{10... | collective-permute-start | bytes 32 | tf_op jit(solution)/shard_map/ppermute | solution.py:18
  5.6 13.6 %collective-permute-start.7 = (s32[2]{0:T(128)S(1)}, s32[2]{0:T(128)S(1)}, u32[]{:S(2)}, u32[]{:S(2)}) collective-permute-start(s32[2]{0:T(128)S(1)} %get-tuple-element.27), channel_id=1, source_target_pairs={{0,2},{1,3},{2,4},{3,5},{4,6},{5,7},{6,8},{7,9},{8,10},{9,11},{10,... | collective-permute-start | bytes 32 | tf_op jit(solution)/shard_map/ppermute | solution.py:18
  7.1 14.8 %collective-permute-start.6 = (s32[2]{0:T(128)S(1)}, s32[2]{0:T(128)S(1)}, u32[]{:S(2)}, u32[]{:S(2)}) collective-permute-start(s32[2]{0:T(128)S(1)} %get-tuple-element.28), channel_id=1, source_target_pairs={{0,1},{1,2},{2,3},{3,4},{4,5},{5,6},{6,7},{7,8},{8,9},{9,10},{10,1... | collective-permute-start | bytes 32 | tf_op jit(solution)/shard_map/ppermute | solution.py:18
  7.6 15.9 %collective-permute-start.2 = (s32[2]{0:T(128)S(1)}, s32[2]{0:T(128)S(1)}, u32[]{:S(2)}, u32[]{:S(2)}) collective-permute-start(s32[2]{0:T(128)S(1)} %get-tuple-element.30), channel_id=1, source_target_pairs={{0,3},{1,4},{2,5},{3,6},{4,7},{5,8},{6,9},{7,10},{8,11},{9,12},{10... | collective-permute-start | bytes 32 | tf_op jit(solution)/shard_map/ppermute | solution.py:18
  9.9 13.6 %collective-permute-start.1 = (s32[2]{0:T(128)S(1)}, s32[2]{0:T(128)S(1)}, u32[]{:S(2)}, u32[]{:S(2)}) collective-permute-start(s32[2]{0:T(128)S(1)} %get-tuple-element.31), channel_id=1, source_target_pairs={{0,2},{1,3},{2,4},{3,5},{4,6},{5,7},{6,8},{7,9},{8,10},{9,11},{10,... | collective-permute-start | bytes 32 | tf_op jit(solution)/shard_map/ppermute | solution.py:18
  15.3 16.5 %copy-start.5 = (f32[8,2,128]{2,1,0:T(2,128)S(1)}, f32[8,2,128]{2,1,0:T(2,128)}, u32[]{:S(2)}) copy-start(f32[8,2,128]{2,1,0:T(2,128)} %fusion.53) | copy-start | bytes 24580
  19.2 6.6 %collective-permute-start = (s32[2]{0:T(128)S(1)}, s32[2]{0:T(128)S(1)}, u32[]{:S(2)}, u32[]{:S(2)}) collective-permute-start(s32[2]{0:T(128)S(1)} %get-tuple-element.32), channel_id=1, source_target_pairs={{0,1},{1,2},{2,3},{3,4},{4,5},{5,6},{6,7},{7,8},{8,9},{9,10},{10,1... | collective-permute-start | bytes 32 | tf_op jit(solution)/shard_map/ppermute | solution.py:18
  19.2 6.8 %collective-permute-start.5 = (bf16[2,16384]{1,0:T(2,128)(2,1)S(1)}, bf16[2,16384]{1,0:T(2,128)(2,1)S(1)}, u32[]{:S(2)}, u32[]{:S(2)}) collective-permute-start(bf16[2,16384]{1,0:T(2,128)(2,1)S(1)} %get-tuple-element.18), channel_id=1, source_target_pairs={{0,3},{1,4},{2,5},{3,6},{4,7},{5,8},{6,9},{7,10},{8,11},{9,12},{10... | collective-permute-start | bytes 196616 | tf_op jit(solution)/shard_map/ppermute | solution.py:18
  21.9 7.9 %collective-permute-start.4 = (bf16[2,16384]{1,0:T(2,128)(2,1)S(1)}, bf16[2,16384]{1,0:T(2,128)(2,1)S(1)}, u32[]{:S(2)}, u32[]{:S(2)}) collective-permute-start(bf16[2,16384]{1,0:T(2,128)(2,1)S(1)} %get-tuple-element.19), channel_id=1, source_target_pairs={{0,2},{1,3},{2,4},{3,5},{4,6},{5,7},{6,8},{7,9},{8,10},{9,11},{10,... | collective-permute-start | bytes 196616 | tf_op jit(solution)/shard_map/ppermute | solution.py:18
  23.5 7.3 %collective-permute-start.3 = (bf16[2,16384]{1,0:T(2,128)(2,1)S(1)}, bf16[2,16384]{1,0:T(2,128)(2,1)S(1)}, u32[]{:S(2)}, u32[]{:S(2)}) collective-permute-start(bf16[2,16384]{1,0:T(2,128)(2,1)S(1)} %get-tuple-element.20), channel_id=1, source_target_pairs={{0,1},{1,2},{2,3},{3,4},{4,5},{5,6},{6,7},{7,8},{8,9},{9,10},{10,1... | collective-permute-start | bytes 196616 | tf_op jit(solution)/shard_map/ppermute | solution.py:18
  32.2 51.3 %copy-start.3 = (bf16[8,4096]{1,0:T(8,128)(2,1)}, bf16[8,4096]{1,0:T(8,128)(2,1)S(1)}, u32[]{:S(2)}) copy-start(bf16[8,4096]{1,0:T(8,128)(2,1)S(1)} %get-tuple-element.14) | copy-start | bytes 196612
  32.7 52.1 %copy-start.6 = (bf16[1,4096,384]{2,1,0:T(8,128)(2,1)S(1)}, bf16[1,4096,384]{2,1,0:T(8,128)(2,1)}, u32[]{:S(2)}) copy-start(bf16[1,4096,384]{2,1,0:T(8,128)(2,1)} %param.23) | copy-start | bytes 9437188
  83.6 1.3 copy-start.1
  93.3 52.6 %all-to-all-start.1 = ((bf16[32,8,4096]{2,1,0:T(8,128)(2,1)}), bf16[32,8,4096]{2,1,0:T(8,128)(2,1)}, u32[]{:S(2)}, u32[]{:S(2)}) async-start(bf16[32,8,4096]{2,1,0:T(8,128)(2,1)} %fusion), calls=%async_computation.1 | async-start | bytes 4194304 | tf_op jit(solution)/shard_map/all_to_all | solution.py:144
  145.9 2.1 %copy-start.4 = (bf16[8,128]{1,0:T(8,128)(2,1)S(1)}, bf16[8,128]{1,0:T(8,128)(2,1)}, u32[]{:S(2)}) copy-start(bf16[8,128]{1,0:T(8,128)(2,1)} %get-tuple-element.9) | copy-start | bytes 6148
where the time goes:
time: 149 us
  waiting for transfers between devices  55.1 us (37%)
  blocking collectives  50.6 us (34%)
  starting transfers between devices  16 us (11%)
  matrix products  12 us (8%)
  other arithmetic  9.09 us (6%)
  local copies, waits for them, and re-layouts  5.35 us (4%)
    all_to_all x1, blocking collectives, shards(): lax.all_to_all(doubled, 'ep', split_axis=0, concat_axis=0, tiled=True)  50.6 us
    all_to_all x1, waiting for transfers between devices, shards(): lax.all_to_all(partial_value.reshape(device_count, slot_count, width), 'e...  48.1 us
    ppermute x9, starting transfers between devices, from_behind(): lax.ppermute(array, axis, [(i, (i + by) % peers) for i in range(peers)])  12.3 us
    ppermute x9, waiting for transfers between devices, from_behind(): lax.ppermute(array, axis, [(i, (i + by) % peers) for i in range(peers)])  7.01 us
    dot_general x1, matrix products, expert_half(): jnp.dot(hidden, down_matrix, preferred_element_type=jnp.float32)  6.37 us
    all_to_all x1, starting transfers between devices, shards(): lax.all_to_all(partial_value.reshape(device_count, slot_count, width), 'e...  3.7 us
    unnamed x18, local copies, waits for them, and re-layouts  3.21 us
  transfers between devices with their start and end apart: 10, of which 4 were waited for; matrix products, arithmetic and copies ran while one was open for 6% of the time, Pallas kernels for 0%

commit v1 on v0

--- a/solution.py
+++ b/solution.py
@@ -55,7 +55,7 @@
     gate_part = jnp.dot(row_block, gate_matrix, preferred_element_type=jnp.float32)
     up_part = jnp.dot(row_block, up_matrix, preferred_element_type=jnp.float32)
     hidden = (jax.nn.silu(gate_part) * up_part).astype(jnp.bfloat16)
-    return jnp.dot(hidden, down_matrix, preferred_element_type=jnp.float32).astype(jnp.bfloat16)
+    return jnp.dot(hidden, down_matrix, preferred_element_type=jnp.float32)
 
 
 def order_matrix(dest_device, device_count, owned_count, group_rows):
@@ -119,40 +119,20 @@
     summed_state = resid_rows.astype(jnp.float32) + context.astype(jnp.float32)
     inverse = lax.rsqrt(jnp.mean(summed_state * summed_state, axis=1, keepdims=True) + 1e-06)
     normed = (summed_state * inverse * norm_gain.astype(jnp.float32)[None, :]).astype(jnp.bfloat16)
-    width = normed.shape[1]
     experts = device_count // 2
-    capacity = 2 * max(1, min(owned_count // 2, owned_count * TOPK // experts))
-    flat_ids = route_ids.reshape(-1)
-    onehot = (flat_ids[:, None] == jnp.arange(experts, dtype=jnp.int32)[None, :]).astype(jnp.int32)
-    slot_index = jnp.sum((jnp.cumsum(onehot, axis=0) - onehot) * onehot, axis=1)
-    position = flat_ids * capacity + slot_index
-    hit_table = (
-        position[:, None] == jnp.arange(experts * capacity, dtype=jnp.int32)[None, :]
-    ).reshape(owned_count, TOPK, -1)
-    gather_rows = jnp.sum(hit_table.astype(jnp.float32), axis=1).astype(jnp.bfloat16)
-    blend_matrix = jnp.sum(
-        jnp.where(hit_table, route_weight.astype(jnp.float32)[:, :, None], 0.0), axis=1
+    hits = route_ids[:, :, None] == jnp.arange(experts, dtype=jnp.int32)[None, None, :]
+    table = jnp.sum(
+        jnp.where(hits, route_weight.astype(jnp.float32)[:, :, None], 0.0), axis=1
     ).astype(jnp.bfloat16)
-    outgoing_rows = apply_rows(gather_rows.T, normed)
-    doubled = jnp.broadcast_to(
-        outgoing_rows.reshape(experts, 1, capacity, width), (experts, 2, capacity, width)
+    all_tables = lax.all_gather(table, "ep", axis=0, tiled=True)
+    mine = jnp.arange(experts, dtype=jnp.int32) == lax.axis_index("ep") // 2
+    share = jnp.sum(
+        jnp.where(mine[None, :], all_tables.astype(jnp.float32), 0.0), axis=1, keepdims=True
     )
-    doubled = doubled.reshape(device_count, capacity, width)
-    arrived = lax.all_to_all(doubled, "ep", split_axis=0, concat_axis=0, tiled=True)
-    slot_count = arrived.shape[1]
-    partial_value = expert_half(arrived.reshape(-1, width), w_gate[0], w_up[0], w_down[0])
-    returned = lax.all_to_all(
-        partial_value.reshape(device_count, slot_count, width),
-        "ep",
-        split_axis=0,
-        concat_axis=0,
-        tiled=True,
-    )
-    halves = returned.reshape(experts, 2, capacity, width).astype(jnp.float32)
-    expert_out = (
-        (halves[:, 0] + halves[:, 1]).astype(jnp.bfloat16).reshape(experts * capacity, width)
-    )
-    moe_out = apply_rows(blend_matrix, expert_out)
+    all_rows = lax.all_gather(normed, "ep", axis=0, tiled=True)
+    partial_value = expert_half(all_rows, w_gate[0], w_up[0], w_down[0])
+    weighted = (partial_value * share).astype(jnp.bfloat16)
+    moe_out = lax.psum_scatter(weighted, "ep", scatter_dimension=0, tiled=True)
     return (moved_cache, context, moe_out)
 
 

time: 149 us -> 242 us (1.62)
  waiting for transfers between devices: 55.1 us -> 157 us
  blocking collectives: 50.6 us -> 37 us
  between operations: 0.84 us -> 14.3 us
  other arithmetic: 9.09 us -> 4.91 us
  starting transfers between devices: 16 us -> 12.4 us
    reduce_scatter x0 -> x1, waiting for transfers between devices: none -> 135 us  [shards(): moe_out = lax.psum_scatter(weighted, 'ep', scatter_dimension=0, tiled=True)]
    all_to_all x1 -> x0, blocking collectives: 50.6 us -> none  [shards(): lax.all_to_all(doubled, 'ep', split_axis=0, concat_axis=0, tiled=True)]
    all_to_all x1 -> x0, waiting for transfers between devices: 48.1 us -> none  [shards(): lax.all_to_all(partial_value.reshape(device_count, slot_count, width), 'e...]
    all_gather x0 -> x1, blocking collectives: none -> 37 us  [shards(): all_tables = lax.all_gather(table, 'ep', axis=0, tiled=True)]
    all_gather x0 -> x1, waiting for transfers between devices: none -> 15.6 us  [shards(): all_rows = lax.all_gather(normed, 'ep', axis=0, tiled=True)]
    all_to_all x1 -> x0, starting transfers between devices: 3.7 us -> none  [shards(): lax.all_to_all(partial_value.reshape(device_count, slot_count, width), 'e...]
    dot_general x1, matrix products: 2.09 us -> 4.53 us  [expert_half(): jnp.dot(row_block, gate_matrix, preferred_element_type=jnp.float32)]
  transfers between devices with their start and end apart: 10 -> 11, of which waited for: 4 -> 5; matrix products, arithmetic and copies ran while one was open for 6% -> 2% of each run, Pallas kernels for 0% -> 0%
where the time goes in v1:
time: 242 us
  waiting for transfers between devices  157 us (65%)
  blocking collectives  37 us (15%)
  between operations  14.3 us (6%)
  matrix products  13 us (5%)
  starting transfers between devices  12.4 us (5%)
  other arithmetic  4.91 us (2%)
  local copies, waits for them, and re-layouts  2.98 us (1%)
    reduce_scatter x1, waiting for transfers between devices, shards(): moe_out = lax.psum_scatter(weighted, 'ep', scatter_dimension=0, tiled=True)  135 us
    all_gather x1, blocking collectives, shards(): all_tables = lax.all_gather(table, 'ep', axis=0, tiled=True)  37 us
    all_gather x1, waiting for transfers between devices, shards(): all_rows = lax.all_gather(normed, 'ep', axis=0, tiled=True)  15.6 us
    ppermute x9, starting transfers between devices, from_behind(): lax.ppermute(array, axis, [(i, (i + by) % peers) for i in range(peers)])  12.3 us
    ppermute x9, waiting for transfers between devices, from_behind(): lax.ppermute(array, axis, [(i, (i + by) % peers) for i in range(peers)])  7.01 us
    dot_general x1, matrix products, expert_half(): return jnp.dot(hidden, down_matrix, preferred_element_type=jnp.float32)  6.3 us
  transfers between devices with their start and end apart: 11, of which 5 were waited for; matrix products, arithmetic and copies ran while one was open for 2% of the time, Pallas kernels for 0%

profile of v1, /device:TPU:0, one launch (start us, length us, event | category | flops | bytes accessed | tf_op | source)
XLA Modules:
  0.0 241.6 jit_solution(17856734830505190898)
XLA Ops:
  7.3 0.8 and_select_fusion
  8.3 0.7 multiply_add_fusion
  9.0 0.8 select_reduce_fusion.4
  9.9 2.4 collective-permute-start.8
  12.2 1.5 collective-permute-start.7
  13.7 0.4 collective-permute-start.6
  14.2 2.3 collective-permute-start.2
  16.5 1.5 collective-permute-start.1
  18.0 0.7 slice_bitcast_fusion
  18.7 0.7 convert_element_type.77
  19.4 1.1 copy.33
  20.9 1.0 fusion.34
  22.0 2.7 %collective-permute-start.5 = (bf16[2,16384]{1,0:T(2,128)(2,1)S(1)}, bf16[2,16384]{1,0:T(2,128)(2,1)S(1)}, u32[]{:S(2)}, u32[]{:S(2)}) collective-permute-start(bf16[2,16384]{1,0:T(2,128)(2,1)S(1)} %get-tuple-element.16), channel_id=1, source_target_pairs={{0,3},{1,4},{2,5},{3,6},{4,7},{5,8},{6,9},{7,10},{8,11},{9,12},{10... | collective-permute-start | bytes 196616 | tf_op jit(solution)/shard_map/ppermute | solution.py:18
  24.7 1.5 collective-permute-start.4
  26.3 2.3 collective-permute-done
  28.8 3.7 %collective-permute-done.4 = bf16[2,16384]{1,0:T(2,128)(2,1)S(1)} collective-permute-done((bf16[2,16384]{1,0:T(2,128)(2,1)S(1)}, bf16[2,16384]{1,0:T(2,128)(2,1)S(1)}, u32[]{:S(2)}, u32[]{:S(2)}) %collective-permute-start.4) | collective-permute-done | bytes 65568 | tf_op jit(solution)/shard_map/ppermute | solution.py:18
  32.5 1.0 collective-permute-done.3
  35.0 0.7 multiply_convert_fusion
  35.9 37.0 %all_gather.7 = bf16[256,16]{1,0:T(8,128)(2,1)S(1)} all-gather(bf16[8,16]{1,0:T(8,128)(2,1)S(1)} %select_reduce_fusion.2), channel_id=1, replica_groups=mesh['groups'=1,'ep'=32] {'ep'}, dimensions={0}, use_global_device_ids=true | all-gather | bytes 8448 | tf_op jit(solution)/shard_map/all_gather | solution.py:127
  73.0 15.6 %all-gather.2.cloned.1.call-done = bf16[256,4096]{1,0:T(8,128)(2,1)} async-done(((bf16[8,4096]{1,0:T(8,128)(2,1)}), bf16[256,4096]{1,0:T(8,128)(2,1)}) %all-gather.2.cloned.1.call-update) | async-done | bytes 2097168 | tf_op jit(solution)/shard_map/all_gather | solution.py:132
  88.6 4.5 %fusion.4 = f32[256,384]{1,0:T(8,128)} fusion(bf16[256,4096]{1,0:T(8,128)(2,1)} %all-gather.2.cloned.1.call-done, bf16[1,4096,384]{2,1,0:T(8,128)(2,1)} %param.23), kind=kOutput, calls=%fused_computation.7 | convolution fusion | flops 805306368 | bytes 5636096 | tf_op jit(solution)/shard_map/dot_general | solution.py:55
  93.2 6.3 %fusion = bf16[256,4096]{1,0:T(8,128)(2,1)} fusion(bf16[1,384,4096]{2,1,0:T(8,128)(2,1)S(1)} %copy-done, f32[256]{0:T(256)S(1)} %select_reduce_fusion, bf16[256,4096]{1,0:T(8,128)(2,1)} %all-gather.2.cloned.1.call-done, bf16[1,4096,384]{2,1,0:T(8,128)(2,1)} %param.24, f32[256,384]{1,0:T(8,128)} %fusion.4), kind=kOutput, calls=%fused_computation.3 | convolution fusion | flops 1613299712 | bytes 10880000 | tf_op jit(solution)/shard_map/dot_general | solution.py:58
  99.5 0.8 copy.26
  100.3 134.5 %reduce-scatter.2.cloned.1.call-done = bf16[8,4096]{1,0:T(8,128)(2,1)} async-done(((bf16[256,4096]{1,0:T(8,128)(2,1)}), bf16[8,4096]{1,0:T(8,128)(2,1)}) %reduce-scatter.2.cloned.1.call-update) | async-done | bytes 65552 | tf_op jit(solution)/shard_map/reduce_scatter | solution.py:135
  (50 shorter events, 2.9 us)
Async XLA Ops:
  7.2 86.0 %copy-start = (bf16[1,384,4096]{2,1,0:T(8,128)(2,1)S(1)}, bf16[1,384,4096]{2,1,0:T(8,128)(2,1)}, u32[]{:S(2)}) copy-start(bf16[1,384,4096]{2,1,0:T(8,128)(2,1)} %param.25) | copy-start | bytes 9437188
  7.2 26.8 %copy-start.5 = (bf16[8,4096]{1,0:T(8,128)(2,1)S(1)}, bf16[8,4096]{1,0:T(8,128)(2,1)}, u32[]{:S(2)}) copy-start(bf16[8,4096]{1,0:T(8,128)(2,1)} %param.17) | copy-start | bytes 196612
  7.2 27.6 %copy-start.1 = (bf16[8,4096]{1,0:T(8,128)(2,1)S(1)}, bf16[8,4096]{1,0:T(8,128)(2,1)}, u32[]{:S(2)}) copy-start(bf16[8,4096]{1,0:T(8,128)(2,1)} %param.19) | copy-start | bytes 196612
  7.2 28.6 %copy-start.4 = (bf16[8,8]{1,0:T(8,128)(2,1)S(1)}, bf16[8,8]{1,0:T(8,128)(2,1)}, u32[]{:S(2)}) copy-start(bf16[8,8]{1,0:T(8,128)(2,1)} %param.22) | copy-start | bytes 388
  7.2 28.6 %copy-start.3 = (s32[8,8]{1,0:T(8,128)S(1)}, s32[8,8]{1,0:T(8,128)}, u32[]{:S(2)}) copy-start(s32[8,8]{1,0:T(8,128)} %param.21) | copy-start | bytes 772
  7.2 81.4 %all-gather.2.cloned.1.call-start = ((), (), s32[]{:S(2)}) async-start(), calls=%async_computation.1 | async-start | bytes 2162688 | tf_op jit(solution)/shard_map/all_gather | solution.py:132
  9.9 12.1 %collective-permute-start.8 = (s32[2]{0:T(128)S(1)}, s32[2]{0:T(128)S(1)}, u32[]{:S(2)}, u32[]{:S(2)}) collective-permute-start(s32[2]{0:T(128)S(1)} %get-tuple-element.24), channel_id=1, source_target_pairs={{0,3},{1,4},{2,5},{3,6},{4,7},{5,8},{6,9},{7,10},{8,11},{9,12},{10... | collective-permute-start | bytes 32 | tf_op jit(solution)/shard_map/ppermute | solution.py:18
  12.2 9.8 %collective-permute-start.7 = (s32[2]{0:T(128)S(1)}, s32[2]{0:T(128)S(1)}, u32[]{:S(2)}, u32[]{:S(2)}) collective-permute-start(s32[2]{0:T(128)S(1)} %get-tuple-element.25), channel_id=1, source_target_pairs={{0,2},{1,3},{2,4},{3,5},{4,6},{5,7},{6,8},{7,9},{8,10},{9,11},{10,... | collective-permute-start | bytes 32 | tf_op jit(solution)/shard_map/ppermute | solution.py:18
  13.7 11.0 %collective-permute-start.6 = (s32[2]{0:T(128)S(1)}, s32[2]{0:T(128)S(1)}, u32[]{:S(2)}, u32[]{:S(2)}) collective-permute-start(s32[2]{0:T(128)S(1)} %get-tuple-element.26), channel_id=1, source_target_pairs={{0,1},{1,2},{2,3},{3,4},{4,5},{5,6},{6,7},{7,8},{8,9},{9,10},{10,1... | collective-permute-start | bytes 32 | tf_op jit(solution)/shard_map/ppermute | solution.py:18
  14.2 12.0 %collective-permute-start.2 = (s32[2]{0:T(128)S(1)}, s32[2]{0:T(128)S(1)}, u32[]{:S(2)}, u32[]{:S(2)}) collective-permute-start(s32[2]{0:T(128)S(1)} %get-tuple-element.28), channel_id=1, source_target_pairs={{0,3},{1,4},{2,5},{3,6},{4,7},{5,8},{6,9},{7,10},{8,11},{9,12},{10... | collective-permute-start | bytes 32 | tf_op jit(solution)/shard_map/ppermute | solution.py:18
  16.5 9.8 %collective-permute-start.1 = (s32[2]{0:T(128)S(1)}, s32[2]{0:T(128)S(1)}, u32[]{:S(2)}, u32[]{:S(2)}) collective-permute-start(s32[2]{0:T(128)S(1)} %get-tuple-element.29), channel_id=1, source_target_pairs={{0,2},{1,3},{2,4},{3,5},{4,6},{5,7},{6,8},{7,9},{8,10},{9,11},{10,... | collective-permute-start | bytes 32 | tf_op jit(solution)/shard_map/ppermute | solution.py:18
  21.9 6.6 %collective-permute-start = (s32[2]{0:T(128)S(1)}, s32[2]{0:T(128)S(1)}, u32[]{:S(2)}, u32[]{:S(2)}) collective-permute-start(s32[2]{0:T(128)S(1)} %get-tuple-element.30), channel_id=1, source_target_pairs={{0,1},{1,2},{2,3},{3,4},{4,5},{5,6},{6,7},{7,8},{8,9},{9,10},{10,1... | collective-permute-start | bytes 32 | tf_op jit(solution)/shard_map/ppermute | solution.py:18
  22.0 6.8 %collective-permute-start.5 = (bf16[2,16384]{1,0:T(2,128)(2,1)S(1)}, bf16[2,16384]{1,0:T(2,128)(2,1)S(1)}, u32[]{:S(2)}, u32[]{:S(2)}) collective-permute-start(bf16[2,16384]{1,0:T(2,128)(2,1)S(1)} %get-tuple-element.16), channel_id=1, source_target_pairs={{0,3},{1,4},{2,5},{3,6},{4,7},{5,8},{6,9},{7,10},{8,11},{9,12},{10... | collective-permute-start | bytes 196616 | tf_op jit(solution)/shard_map/ppermute | solution.py:18
  24.7 7.9 %collective-permute-start.4 = (bf16[2,16384]{1,0:T(2,128)(2,1)S(1)}, bf16[2,16384]{1,0:T(2,128)(2,1)S(1)}, u32[]{:S(2)}, u32[]{:S(2)}) collective-permute-start(bf16[2,16384]{1,0:T(2,128)(2,1)S(1)} %get-tuple-element.17), channel_id=1, source_target_pairs={{0,2},{1,3},{2,4},{3,5},{4,6},{5,7},{6,8},{7,9},{8,10},{9,11},{10,... | collective-permute-start | bytes 196616 | tf_op jit(solution)/shard_map/ppermute | solution.py:18
  26.3 7.3 %collective-permute-start.3 = (bf16[2,16384]{1,0:T(2,128)(2,1)S(1)}, bf16[2,16384]{1,0:T(2,128)(2,1)S(1)}, u32[]{:S(2)}, u32[]{:S(2)}) collective-permute-start(bf16[2,16384]{1,0:T(2,128)(2,1)S(1)} %get-tuple-element.18), channel_id=1, source_target_pairs={{0,1},{1,2},{2,3},{3,4},{4,5},{5,6},{6,7},{7,8},{8,9},{9,10},{10,1... | collective-permute-start | bytes 196616 | tf_op jit(solution)/shard_map/ppermute | solution.py:18
  35.0 58.2 %copy-start.2 = (bf16[8,4096]{1,0:T(8,128)(2,1)}, bf16[8,4096]{1,0:T(8,128)(2,1)S(1)}, u32[]{:S(2)}) copy-start(bf16[8,4096]{1,0:T(8,128)(2,1)S(1)} %get-tuple-element.12) | copy-start | bytes 196612
  35.7 199.1 %reduce-scatter.2.cloned.1.call-start = ((), (), s32[]{:S(2)}) async-start(), calls=%async_computation.2 | async-start | bytes 2162688 | tf_op jit(solution)/shard_map/reduce_scatter | solution.py:135
Sparse Core Ops, SparseCore 0:
  35.9 52.7 all-gather.1
  99.6 135.1 reduce-scatter.1

commit v2 on v1

--- a/solution.py
+++ b/solution.py
@@ -1,8 +1,11 @@
+import functools
 import math
 
 import jax
 import jax.numpy as jnp
 from jax import lax
+from jax.experimental import pallas as pl
+from jax.experimental.pallas import tpu as pltpu
 from jax.sharding import PartitionSpec as P
 
 HEAD_DIM = 128
@@ -51,11 +54,319 @@
     return context.reshape(row_count, Q_HEADS * HEAD_DIM).astype(jnp.bfloat16)
 
 
-def expert_half(row_block, gate_matrix, up_matrix, down_matrix):
-    gate_part = jnp.dot(row_block, gate_matrix, preferred_element_type=jnp.float32)
-    up_part = jnp.dot(row_block, up_matrix, preferred_element_type=jnp.float32)
-    hidden = (jax.nn.silu(gate_part) * up_part).astype(jnp.bfloat16)
-    return jnp.dot(hidden, down_matrix, preferred_element_type=jnp.float32)
+TABLE = 256
+
+
+def bit_orders(bits):
+    down = list(reversed(range(bits)))
+    swapped = down[:-2] + [down[-1], down[-2]]
+    early = [0, 1] + list(reversed(range(2, bits)))
+    return (down, swapped, early)
+
+
+def relative(order, place):
+    return sum(1 << order[j] for j in range(len(order)) if place >> j & 1)
+
+
+def widths(half):
+    tiles = half // 128
+    first = (tiles - 2) // 3
+    second = (tiles - first) // 2
+    gather = (first * 128, second * 128, (tiles - first - second) * 128)
+    third = tiles // 3
+    rest = (tiles - third) // 2
+    scatter = (third * 128, rest * 128, (tiles - third - rest) * 128)
+    return gather, scatter
+
+
+def fold_wide(value):
+    cut = value.shape[1] // 2
+    return jnp.concatenate([value[:, :cut], value[:, cut:]], axis=0)
+
+
+def unfold_wide(value):
+    cut = value.shape[0] // 2
+    return jnp.concatenate([value[:cut], value[cut:]], axis=1)
+
+
+def expert_kernel(
+    bits,
+    folded_ref,
+    gate_hbm,
+    up_hbm,
+    down_hbm,
+    out_ref,
+    gate_ref,
+    up_ref,
+    down_ref,
+    stage,
+    last_send,
+    last_recv,
+    gate_sum,
+    up_sum,
+    g0,
+    g1,
+    g2,
+    o0,
+    o1,
+    o2,
+    s0,
+    s1,
+    s2,
+    d0,
+    d1,
+    d2,
+    a0,
+    a1,
+    a2,
+    e0,
+    e1,
+    e2,
+    load_sem,
+    pair_send,
+    pair_recv,
+    step_send,
+    step_recv,
+):
+    chips = 1 << bits
+    width = down_ref.shape[1]
+    half = width // 2
+    gather, scatter = widths(half)
+    orders = bit_orders(bits)
+    held, other = (g0, g1, g2), (o0, o1, o2)
+    given, taken, total, landed = (s0, s1, s2), (d0, d1, d2), (a0, a1, a2), (e0, e1, e2)
+    me = lax.axis_index("ep")
+    chip = me // 2
+    core = me % 2
+    mate = me + 1 - 2 * core
+    far = []
+    for bit in range(bits):
+        own_bit = (chip // (1 << bit)) % 2
+        far.append(me + (1 - 2 * own_bit) * (2 << bit))
+
+    loads = []
+    for k, (src, dst) in enumerate(
+        ((gate_hbm, gate_ref), (up_hbm, up_ref), (down_hbm, down_ref))
+    ):
+        load = pltpu.make_async_copy(src.at[0], dst, load_sem.at[k])
+        load.start()
+        loads.append(load)
+
+    barrier = pltpu.get_barrier_semaphore()
+    for target in [mate] + far:
+        pl.semaphore_signal(barrier, inc=1, device_id={"ep": target})
+    pl.semaphore_wait(barrier, 1 + bits)
+
+    def send(src, dst, send_sem, recv_sem, target):
+        copy = pltpu.make_async_remote_copy(
+            src_ref=src,
+            dst_ref=dst,
+            send_sem=send_sem,
+            recv_sem=recv_sem,
+            device_id={"ep": target},
+        )
+        copy.start()
+        return copy
+
+    sent = []
+    first = send(folded_ref.at[1 - core], stage, pair_send.at[0], pair_recv.at[0], mate)
+    sent.append(first)
+    mine = unfold_wide(folded_ref[core].astype(jnp.float32))
+    first.wait_recv()
+    theirs = unfold_wide(stage[...].astype(jnp.float32))
+    block = jnp.where(
+        core == 0,
+        jnp.concatenate([mine, theirs], axis=0),
+        jnp.concatenate([theirs, mine], axis=0),
+    ).astype(jnp.bfloat16)
+    starts = (0, gather[0], gather[0] + gather[1])
+    held[0][0] = jnp.concatenate(
+        [block[:, : gather[0]], block[:, half:]], axis=1
+    )
+    for c in (1, 2):
+        held[c][0] = block[:, starts[c] : starts[c] + gather[c]]
+
+    steps = {}
+    for i in range(bits):
+        count = 1 << i
+        for c in range(3):
+            if i > 0:
+                steps[c, i - 1].wait_recv()
+            steps[c, i] = send(
+                held[c].at[pl.ds(0, count)],
+                held[c].at[pl.ds(count, count)],
+                step_send.at[c * bits + i],
+                step_recv.at[c * bits + i],
+                far[orders[c][i]],
+            )
+            sent.append(steps[c, i])
+    loads[0].wait()
+    loads[1].wait()
+
+    def operand(buffer, c):
+        place = {relative(orders[c], p): p for p in range(chips)}
+        return jnp.concatenate([buffer[place[r]] for r in range(chips)], axis=0)
+
+    def accumulate(rows, c, side, fresh):
+        base = pl.multiple_of(side * half + starts[c], 128)
+        left = rows[:, : gather[c]]
+        g = jnp.dot(
+            left, gate_ref[pl.ds(base, gather[c]), :], preferred_element_type=jnp.float32
+        )
+        u = jnp.dot(
+            left, up_ref[pl.ds(base, gather[c]), :], preferred_element_type=jnp.float32
+        )
+        if fresh:
+            gate_sum[...] = g
+            up_sum[...] = u
+        else:
+            gate_sum[...] += g
+            up_sum[...] += u
+
+    swaps = []
+    share = None
+    for c in range(3):
+        steps[c, bits - 1].wait_recv()
+        swap = send(held[c], other[c], pair_send.at[1 + c], pair_recv.at[1 + c], mate)
+        swaps.append(swap)
+        sent.append(swap)
+        rows = operand(held[c], c)
+        if c == 0:
+            tables = rows[:, gather[0] :].astype(jnp.float32)
+            lane = lax.broadcasted_iota(jnp.int32, tables.shape, 1)
+            share = jnp.sum(jnp.where(lane == chip, tables, 0.0), axis=1, keepdims=True)
+        accumulate(rows, c, core, c == 0)
+    for c in range(3):
+        swaps[c].wait_recv()
+        accumulate(operand(other[c], c), c, 1 - core, False)
+
+    gate = gate_sum[...]
+    hidden = (gate * jax.nn.sigmoid(gate) * up_sum[...]).astype(jnp.bfloat16)
+    loads[2].wait()
+    begins = (0, scatter[0], scatter[0] + scatter[1])
+
+    def down(c, side):
+        base = pl.multiple_of(side * half + begins[c], 128)
+        return (
+            jnp.dot(
+                hidden, down_ref[:, pl.ds(base, scatter[c])], preferred_element_type=jnp.float32
+            )
+            * share
+        )
+
+    trades = []
+    for c in range(3):
+        value = down(c, 1 - core).astype(jnp.bfloat16)
+        for p in range(chips):
+            r = relative(orders[c], p)
+            given[c][p] = value[16 * r : 16 * r + 16]
+        trade = send(given[c], taken[c], pair_send.at[4 + c], pair_recv.at[4 + c], mate)
+        trades.append(trade)
+        sent.append(trade)
+    base_sem = 3 * bits
+    backs = {}
+
+    def back(c, i):
+        count = 1 << i
+        backs[c, i] = send(
+            total[c].at[pl.ds(count, count)],
+            landed[c].at[pl.ds(count, count)],
+            step_send.at[base_sem + c * bits + i],
+            step_recv.at[base_sem + c * bits + i],
+            far[orders[c][i]],
+        )
+        sent.append(backs[c, i])
+
+    for c in range(3):
+        value = down(c, core)
+        trades[c].wait_recv()
+        for p in reversed(range(chips)):
+            r = relative(orders[c], p)
+            total[c][p] = (
+                value[16 * r : 16 * r + 16] + taken[c][p].astype(jnp.float32)
+            ).astype(jnp.bfloat16)
+        back(c, bits - 1)
+    ends = []
+    for i in reversed(range(bits)):
+        count = 1 << i
+        for c in range(3):
+            backs[c, i].wait_recv()
+            value = total[c][0:count].astype(jnp.float32) + landed[c][
+                count : 2 * count
+            ].astype(jnp.float32)
+            if i > 0:
+                total[c][0:count] = value.astype(jnp.bfloat16)
+                back(c, i - 1)
+            else:
+                ends.append(value[0])
+    done = jnp.concatenate(ends, axis=1)
+    rows = done.shape[0] // 2
+    keep = jnp.where(core == 0, done[:rows], done[rows:])
+    pass_on = jnp.where(core == 0, done[rows:], done[:rows])
+    last_send[...] = fold_wide(pass_on).astype(jnp.bfloat16)
+    final = send(last_send, last_recv, pair_send.at[7], pair_recv.at[7], mate)
+    sent.append(final)
+    final.wait_recv()
+    got = unfold_wide(last_recv[...].astype(jnp.float32))
+    out_ref[...] = jnp.where(
+        core == 0,
+        jnp.concatenate([keep, got], axis=1),
+        jnp.concatenate([got, keep], axis=1),
+    ).astype(out_ref.dtype)
+    for copy in sent:
+        copy.wait_send()
+
+
+def expert_layer(normed, table, w_gate, w_up, w_down):
+    devices = lax.axis_size("ep")
+    bits = (devices // 2).bit_length() - 1
+    chips = 1 << bits
+    rows, width = normed.shape
+    half = width // 2
+    gather, scatter = widths(half)
+    padded = jnp.pad(table, ((0, 0), (0, TABLE - table.shape[1])))
+    folded = jnp.stack(
+        [
+            fold_wide(jnp.concatenate([normed[:, h * half : (h + 1) * half], padded], axis=1))
+            for h in (0, 1)
+        ]
+    )
+    both = 2 * rows
+    bf = jnp.bfloat16
+    gather_shapes = [
+        pltpu.VMEM((chips, both, gather[c] + (TABLE if c == 0 else 0)), bf) for c in range(3)
+    ]
+    scatter_shapes = [pltpu.VMEM((chips, both, scatter[c]), bf) for c in range(3)]
+    hidden_count = w_gate.shape[2]
+    return pl.pallas_call(
+        functools.partial(expert_kernel, bits),
+        out_shape=jax.ShapeDtypeStruct((rows, width), bf),
+        in_specs=[pl.BlockSpec(memory_space=pltpu.VMEM)]
+        + [pl.BlockSpec(memory_space=pl.ANY)] * 3,
+        out_specs=pl.BlockSpec(memory_space=pltpu.VMEM),
+        scratch_shapes=[
+            pltpu.VMEM(w_gate.shape[1:], bf),
+            pltpu.VMEM(w_up.shape[1:], bf),
+            pltpu.VMEM(w_down.shape[1:], bf),
+            pltpu.VMEM((both, (half + TABLE) // 2), bf),
+            pltpu.VMEM((both, half // 2), bf),
+            pltpu.VMEM((both, half // 2), bf),
+            pltpu.VMEM((chips * both, hidden_count), jnp.float32),
+            pltpu.VMEM((chips * both, hidden_count), jnp.float32),
+        ]
+        + gather_shapes * 2
+        + scatter_shapes * 4
+        + [
+            pltpu.SemaphoreType.DMA((3,)),
+            pltpu.SemaphoreType.DMA((8,)),
+            pltpu.SemaphoreType.DMA((8,)),
+            pltpu.SemaphoreType.DMA((6 * bits,)),
+            pltpu.SemaphoreType.DMA((6 * bits,)),
+        ],
+        compiler_params=pltpu.CompilerParams(
+            collective_id=0, has_side_effects=True, vmem_limit_bytes=56 * 1024 * 1024
+        ),
+    )(folded, w_gate, w_up, w_down)
 
 
 def order_matrix(dest_device, device_count, owned_count, group_rows):
@@ -124,15 +435,7 @@
     table = jnp.sum(
         jnp.where(hits, route_weight.astype(jnp.float32)[:, :, None], 0.0), axis=1
     ).astype(jnp.bfloat16)
-    all_tables = lax.all_gather(table, "ep", axis=0, tiled=True)
-    mine = jnp.arange(experts, dtype=jnp.int32) == lax.axis_index("ep") // 2
-    share = jnp.sum(
-        jnp.where(mine[None, :], all_tables.astype(jnp.float32), 0.0), axis=1, keepdims=True
-    )
-    all_rows = lax.all_gather(normed, "ep", axis=0, tiled=True)
-    partial_value = expert_half(all_rows, w_gate[0], w_up[0], w_down[0])
-    weighted = (partial_value * share).astype(jnp.bfloat16)
-    moe_out = lax.psum_scatter(weighted, "ep", scatter_dimension=0, tiled=True)
+    moe_out = expert_layer(normed, table, w_gate, w_up, w_down)
     return (moved_cache, context, moe_out)
 
 

time: 242 us -> 79.8 us (0.33)
  waiting for transfers between devices: 157 us -> 4.68 us
  Pallas kernels: 0 us -> 47.6 us
  blocking collectives: 37 us -> 0 us
  between operations: 14.3 us -> 0.83 us
  matrix products: 13 us -> 2.12 us
    reduce_scatter x1 -> x0, waiting for transfers between devices: 135 us -> none  [shards(): moe_out = lax.psum_scatter(weighted, 'ep', scatter_dimension=0, tiled=True)]
    pallas_call x0 -> x1, Pallas kernels: none -> 47.6 us  [expert_layer(): pl.pallas_call(functools.partial(expert_kernel, bits), out_shape=jax.Shap...]
    all_gather x1 -> x0, blocking collectives: 37 us -> none  [shards(): all_tables = lax.all_gather(table, 'ep', axis=0, tiled=True)]
    all_gather x1 -> x0, waiting for transfers between devices: 15.6 us -> none  [shards(): all_rows = lax.all_gather(normed, 'ep', axis=0, tiled=True)]
    dot_general x2 -> x0, matrix products: 10.8 us -> none  [the longest x1 6.3 us: expert_half(): return jnp.dot(hidden, down_matrix, preferred_element_type=jnp.float32)]
  transfers between devices with their start and end apart: 11 -> 9, of which waited for: 5 -> 2; matrix products, arithmetic and copies ran while one was open for 2% -> 7% of each run, Pallas kernels for 0% -> 0%
where the time goes in v2:
time: 79.8 us; the launch traced here: 79 us
  Pallas kernels  47.6 us (60%)
  starting transfers between devices  13.2 us (17%)
  other arithmetic  6.09 us (8%)
  waiting for transfers between devices  4.68 us (6%)
  local copies, waits for them, and re-layouts  4.45 us (6%)
  matrix products  2.12 us (3%)
  between operations  0.83 us (1%)
    pallas_call x1, Pallas kernels, expert_layer(): pl.pallas_call(functools.partial(expert_kernel, bits), out_shape=jax.Shap...  47.6 us
    ppermute x9, starting transfers between devices, from_behind(): lax.ppermute(array, axis, [(i, (i + by) % peers) for i in range(peers)])  13.2 us
    ppermute x9, waiting for transfers between devices, from_behind(): lax.ppermute(array, axis, [(i, (i + by) % peers) for i in range(peers)])  4.68 us
    unnamed x9, local copies, waits for them, and re-layouts  3.37 us
  transfers between devices with their start and end apart: 9, of which 2 were waited for; matrix products, arithmetic and copies ran while one was open for 7% of the time, Pallas kernels for 0%

profile of v2, /device:TPU:0, one launch (start us, length us, event | category | flops | bytes accessed | tf_op | source)
XLA Modules:
  0.0 79.0 jit_solution(492587492594681101)
XLA Ops:
  0.7 0.7 and_select_fusion
  1.6 0.7 multiply_add_fusion
  2.3 0.8 %select_reduce_fusion.3 = (s32[8]{0:T(128)S(1)}, s32[8]{0:T(128)S(1)}) fusion(s32[8]{0:T(128)} %param.14, s32[8]{0:T(128)S(1)} %get-tuple-element.39, s32[8]{0:T(128)S(1)} %get-tuple-element.40), kind=kLoop, calls=%fused_computation.47 | loop fusion | flops 304 | bytes 160 | tf_op jit(solution)/shard_map/reduce_sum | solution.py:409
  3.1 0.5 collective-permute-start
  3.6 2.5 %collective-permute-start.1 = (s32[2]{0:T(128)S(1)}, s32[2]{0:T(128)S(1)}, u32[]{:S(2)}, u32[]{:S(2)}) collective-permute-start(s32[2]{0:T(128)S(1)} %get-tuple-element.35), channel_id=1, source_target_pairs={{0,2},{1,3},{2,4},{3,5},{4,6},{5,7},{6,8},{7,9},{8,10},{9,11},{10,... | collective-permute-start | bytes 32 | tf_op jit(solution)/shard_map/ppermute | solution.py:21
  6.1 2.4 %collective-permute-start.2 = (s32[2]{0:T(128)S(1)}, s32[2]{0:T(128)S(1)}, u32[]{:S(2)}, u32[]{:S(2)}) collective-permute-start(s32[2]{0:T(128)S(1)} %get-tuple-element.34), channel_id=1, source_target_pairs={{0,3},{1,4},{2,5},{3,6},{4,7},{5,8},{6,9},{7,10},{8,11},{9,12},{10... | collective-permute-start | bytes 32 | tf_op jit(solution)/shard_map/ppermute | solution.py:21
  8.6 1.5 %collective-permute-start.7 = (s32[2]{0:T(128)S(1)}, s32[2]{0:T(128)S(1)}, u32[]{:S(2)}, u32[]{:S(2)}) collective-permute-start(s32[2]{0:T(128)S(1)} %get-tuple-element.31), channel_id=1, source_target_pairs={{0,2},{1,3},{2,4},{3,5},{4,6},{5,7},{6,8},{7,9},{8,10},{9,11},{10,... | collective-permute-start | bytes 32 | tf_op jit(solution)/shard_map/ppermute | solution.py:21
  10.1 1.1 %copy.31 = bf16[1,8,32,512]{3,1,2,0:T(8,128)(2,1)S(1)} copy(bf16[1,8,32,512]{3,2,1,0:T(8,128)(2,1)} %bitcast.43) | data formatting | bytes 524288
  11.6 0.7 slice_bitcast_fusion
  12.3 0.7 convert_element_type.70
  13.0 0.7 convert_element_type.72
  13.7 0.8 select_reduce_fusion.1
  14.5 1.0 %fusion.15 = f32[8,2,1,16]{3,2,1,0:T(1,128)S(1)} fusion(bf16[8,2,16,128]{3,0,2,1:T(8,128)(2,1)} %bitcast.48, bf16[8,2,128,1]{2,0,1,3:T(8,128)(2,1)S(1)} %get-tuple-element.27), kind=kOutput, calls=%fused_computation.30 | convolution fusion | flops 65536 | bytes 70656 | tf_op jit(solution)/shard_map/rgjd,rgd->rgj/dot_general | solution.py:36
  15.5 2.4 %collective-permute-start.8 = (s32[2]{0:T(128)S(1)}, s32[2]{0:T(128)S(1)}, u32[]{:S(2)}, u32[]{:S(2)}) collective-permute-start(s32[2]{0:T(128)S(1)} %get-tuple-element.30), channel_id=1, source_target_pairs={{0,3},{1,4},{2,5},{3,6},{4,7},{5,8},{6,9},{7,10},{8,11},{9,12},{10... | collective-permute-start | bytes 32 | tf_op jit(solution)/shard_map/ppermute | solution.py:21
  18.0 1.5 %collective-permute-start.4 = (bf16[2,16384]{1,0:T(2,128)(2,1)S(1)}, bf16[2,16384]{1,0:T(2,128)(2,1)S(1)}, u32[]{:S(2)}, u32[]{:S(2)}) collective-permute-start(bf16[2,16384]{1,0:T(2,128)(2,1)S(1)} %get-tuple-element.17), channel_id=1, source_target_pairs={{0,2},{1,3},{2,4},{3,5},{4,6},{5,7},{6,8},{7,9},{8,10},{9,11},{10,... | collective-permute-start | bytes 196616 | tf_op jit(solution)/shard_map/ppermute | solution.py:21
  19.6 2.4 %collective-permute-start.5 = (bf16[2,16384]{1,0:T(2,128)(2,1)S(1)}, bf16[2,16384]{1,0:T(2,128)(2,1)S(1)}, u32[]{:S(2)}, u32[]{:S(2)}) collective-permute-start(bf16[2,16384]{1,0:T(2,128)(2,1)S(1)} %get-tuple-element.16), channel_id=1, source_target_pairs={{0,3},{1,4},{2,5},{3,6},{4,7},{5,8},{6,9},{7,10},{8,11},{9,12},{10... | collective-permute-start | bytes 196616 | tf_op jit(solution)/shard_map/ppermute | solution.py:21
  22.2 3.2 %collective-permute-done.3 = bf16[2,16384]{1,0:T(2,128)(2,1)S(1)} collective-permute-done((bf16[2,16384]{1,0:T(2,128)(2,1)S(1)}, bf16[2,16384]{1,0:T(2,128)(2,1)S(1)}, u32[]{:S(2)}, u32[]{:S(2)}) %collective-permute-start.3) | collective-permute-done | bytes 65568 | tf_op jit(solution)/shard_map/ppermute | solution.py:21
  25.4 1.4 %collective-permute-done.4 = bf16[2,16384]{1,0:T(2,128)(2,1)S(1)} collective-permute-done((bf16[2,16384]{1,0:T(2,128)(2,1)S(1)}, bf16[2,16384]{1,0:T(2,128)(2,1)S(1)}, u32[]{:S(2)}, u32[]{:S(2)}) %collective-permute-start.4) | collective-permute-done | bytes 65568 | tf_op jit(solution)/shard_map/ppermute | solution.py:21
  26.9 0.4 convolution_convert_fusion
  27.3 0.3 select_reduce_fusion
  28.5 0.6 pad_maximum_fusion.folded_ref
  29.1 47.6 %shard_map.148 = bf16[8,4096]{1,0:T(8,128)(2,1)} custom-call(bf16[2,16,1152]{2,1,0:T(8,128)(2,1)} %pad_maximum_fusion.folded_ref, bf16[1,4096,384]{2,1,0:T(8,128)(2,1)} %gate_hbm.1, bf16[1,4096,384]{2,1,0:T(8,128)(2,1)} %up_hbm.1, bf16[1,384,4096]{2,1,0:T(8,128)(2,1)} %down_hbm.1), custom_call_target="tpu_custom_call" | custom-call | tf_op jit(solution)/shard_map/pallas_call | solution.py:341
  76.8 0.8 copy.25
  77.6 1.5 %copy.53 = bf16[8,4096]{1,0:T(8,128)(2,1)} copy(bf16[8,4096]{1,0:T(8,128)(2,1)} %shard_map.148) | data formatting | bytes 131072
  (42 shorter events, 2.0 us)
Async XLA Ops:
  0.6 26.7 %copy-start.2 = (bf16[8,4096]{1,0:T(8,128)(2,1)S(1)}, bf16[8,4096]{1,0:T(8,128)(2,1)}, u32[]{:S(2)}) copy-start(bf16[8,4096]{1,0:T(8,128)(2,1)} %param.17) | copy-start | bytes 196612
  0.6 27.5 %copy-start = (bf16[8,4096]{1,0:T(8,128)(2,1)S(1)}, bf16[8,4096]{1,0:T(8,128)(2,1)}, u32[]{:S(2)}) copy-start(bf16[8,4096]{1,0:T(8,128)(2,1)} %param.19) | copy-start | bytes 196612
  3.1 12.4 %collective-permute-start = (s32[2]{0:T(128)S(1)}, s32[2]{0:T(128)S(1)}, u32[]{:S(2)}, u32[]{:S(2)}) collective-permute-start(s32[2]{0:T(128)S(1)} %get-tuple-element.36), channel_id=1, source_target_pairs={{0,1},{1,2},{2,3},{3,4},{4,5},{5,6},{6,7},{7,8},{8,9},{9,10},{10,1... | collective-permute-start | bytes 32 | tf_op jit(solution)/shard_map/ppermute | solution.py:21
  3.6 14.4 %collective-permute-start.1 = (s32[2]{0:T(128)S(1)}, s32[2]{0:T(128)S(1)}, u32[]{:S(2)}, u32[]{:S(2)}) collective-permute-start(s32[2]{0:T(128)S(1)} %get-tuple-element.35), channel_id=1, source_target_pairs={{0,2},{1,3},{2,4},{3,5},{4,6},{5,7},{6,8},{7,9},{8,10},{9,11},{10,... | collective-permute-start | bytes 32 | tf_op jit(solution)/shard_map/ppermute | solution.py:21
  6.1 11.8 %collective-permute-start.2 = (s32[2]{0:T(128)S(1)}, s32[2]{0:T(128)S(1)}, u32[]{:S(2)}, u32[]{:S(2)}) collective-permute-start(s32[2]{0:T(128)S(1)} %get-tuple-element.34), channel_id=1, source_target_pairs={{0,3},{1,4},{2,5},{3,6},{4,7},{5,8},{6,9},{7,10},{8,11},{9,12},{10... | collective-permute-start | bytes 32 | tf_op jit(solution)/shard_map/ppermute | solution.py:21
  8.6 11.0 %collective-permute-start.6 = (s32[2]{0:T(128)S(1)}, s32[2]{0:T(128)S(1)}, u32[]{:S(2)}, u32[]{:S(2)}) collective-permute-start(s32[2]{0:T(128)S(1)} %get-tuple-element.32), channel_id=1, source_target_pairs={{0,1},{1,2},{2,3},{3,4},{4,5},{5,6},{6,7},{7,8},{8,9},{9,10},{10,1... | collective-permute-start | bytes 32 | tf_op jit(solution)/shard_map/ppermute | solution.py:21
  8.6 13.4 %collective-permute-start.7 = (s32[2]{0:T(128)S(1)}, s32[2]{0:T(128)S(1)}, u32[]{:S(2)}, u32[]{:S(2)}) collective-permute-start(s32[2]{0:T(128)S(1)} %get-tuple-element.31), channel_id=1, source_target_pairs={{0,2},{1,3},{2,4},{3,5},{4,6},{5,7},{6,8},{7,9},{8,10},{9,11},{10,... | collective-permute-start | bytes 32 | tf_op jit(solution)/shard_map/ppermute | solution.py:21
  15.5 6.5 %collective-permute-start.8 = (s32[2]{0:T(128)S(1)}, s32[2]{0:T(128)S(1)}, u32[]{:S(2)}, u32[]{:S(2)}) collective-permute-start(s32[2]{0:T(128)S(1)} %get-tuple-element.30), channel_id=1, source_target_pairs={{0,3},{1,4},{2,5},{3,6},{4,7},{5,8},{6,9},{7,10},{8,11},{9,12},{10... | collective-permute-start | bytes 32 | tf_op jit(solution)/shard_map/ppermute | solution.py:21
  18.0 7.5 %collective-permute-start.3 = (bf16[2,16384]{1,0:T(2,128)(2,1)S(1)}, bf16[2,16384]{1,0:T(2,128)(2,1)S(1)}, u32[]{:S(2)}, u32[]{:S(2)}) collective-permute-start(bf16[2,16384]{1,0:T(2,128)(2,1)S(1)} %get-tuple-element.18), channel_id=1, source_target_pairs={{0,1},{1,2},{2,3},{3,4},{4,5},{5,6},{6,7},{7,8},{8,9},{9,10},{10,1... | collective-permute-start | bytes 196616 | tf_op jit(solution)/shard_map/ppermute | solution.py:21
  18.0 8.9 %collective-permute-start.4 = (bf16[2,16384]{1,0:T(2,128)(2,1)S(1)}, bf16[2,16384]{1,0:T(2,128)(2,1)S(1)}, u32[]{:S(2)}, u32[]{:S(2)}) collective-permute-start(bf16[2,16384]{1,0:T(2,128)(2,1)S(1)} %get-tuple-element.17), channel_id=1, source_target_pairs={{0,2},{1,3},{2,4},{3,5},{4,6},{5,7},{6,8},{7,9},{8,10},{9,11},{10,... | collective-permute-start | bytes 196616 | tf_op jit(solution)/shard_map/ppermute | solution.py:21
  19.6 7.3 %collective-permute-start.5 = (bf16[2,16384]{1,0:T(2,128)(2,1)S(1)}, bf16[2,16384]{1,0:T(2,128)(2,1)S(1)}, u32[]{:S(2)}, u32[]{:S(2)}) collective-permute-start(bf16[2,16384]{1,0:T(2,128)(2,1)S(1)} %get-tuple-element.16), channel_id=1, source_target_pairs={{0,3},{1,4},{2,5},{3,6},{4,7},{5,8},{6,9},{7,10},{8,11},{9,12},{10... | collective-permute-start | bytes 196616 | tf_op jit(solution)/shard_map/ppermute | solution.py:21
  28.3 48.5 %copy-start.1 = (bf16[8,4096]{1,0:T(8,128)(2,1)}, bf16[8,4096]{1,0:T(8,128)(2,1)S(1)}, u32[]{:S(2)}) copy-start(bf16[8,4096]{1,0:T(8,128)(2,1)S(1)} %get-tuple-element.45) | copy-start | bytes 196612

commit v3 on v2

--- a/solution.py
+++ b/solution.py
@@ -14,11 +14,6 @@
 TOPK = 8
 SPAN = 4
 LEN = 32
-
-
-def from_behind(array, axis, by):
-    peers = lax.axis_size(axis)
-    return lax.ppermute(array, axis, [(i, (i + by) % peers) for i in range(peers)])
 
 
 def attend(query_rows, new_kv, kv_cache, cache_length):
@@ -369,12 +364,107 @@
     )(folded, w_gate, w_up, w_down)
 
 
-def order_matrix(dest_device, device_count, owned_count, group_rows):
-    offset = (dest_device - lax.axis_index("ep")) % device_count
-    onehot = (offset[:, None] == jnp.arange(SPAN, dtype=jnp.int32)[None, :]).astype(jnp.int32)
-    rank = jnp.sum((jnp.cumsum(onehot, axis=0) - onehot) * onehot, axis=1)
-    position = offset * group_rows + rank
-    return jnp.arange(owned_count, dtype=jnp.int32)[:, None] == position[None, :]
+def migrate_kernel(
+    peers,
+    dest_ref,
+    slot_ref,
+    length_ref,
+    cache_ref,
+    arrived_ref,
+    meta_ref,
+    cache_out,
+    cache_in,
+    meta_out,
+    meta_in,
+    cache_send,
+    cache_recv,
+    meta_send,
+    meta_recv,
+):
+    me = lax.axis_index("ep")
+    owned = cache_ref.shape[0]
+    per = owned // SPAN
+    ahead = [lax.rem(me + o, peers) for o in range(SPAN)]
+    behind = [lax.rem(me + peers - o, peers) for o in range(SPAN)]
+    barrier = pltpu.get_barrier_semaphore()
+    for o in range(1, SPAN):
+        pl.semaphore_signal(barrier, inc=1, device_id={"ep": ahead[o]})
+        pl.semaphore_signal(barrier, inc=1, device_id={"ep": behind[o]})
+
+    counts = [jnp.int32(0)] * SPAN
+    chosen = [[jnp.int32(0)] * per for _ in range(SPAN)]
+    for i in range(owned):
+        gap = dest_ref[i] - me
+        gap = jnp.where(gap < 0, gap + peers, gap)
+        for o in range(SPAN):
+            here = gap == o
+            for k in range(per):
+                chosen[o][k] = jnp.where(here & (counts[o] == k), i, chosen[o][k])
+            counts[o] = counts[o] + here.astype(jnp.int32)
+    lane = lax.broadcasted_iota(jnp.int32, meta_out.shape[1:], 1)
+
+    def describe(o):
+        tile = jnp.zeros(meta_out.shape[1:], jnp.int32)
+        for k in range(per):
+            tile = jnp.where(lane == k, slot_ref[chosen[o][k]], tile)
+            tile = jnp.where(lane == per + k, length_ref[chosen[o][k]], tile)
+        return tile
+
+    for o in range(1, SPAN):
+        for k in range(per):
+            cache_out[o - 1, k] = cache_ref[chosen[o][k]]
+        meta_out[o - 1] = describe(o)
+    pl.semaphore_wait(barrier, 2 * (SPAN - 1))
+    copies = []
+    for o in range(SPAN - 1, 0, -1):
+        for src, dst, send_sem, recv_sem in (
+            (cache_out, cache_in, cache_send, cache_recv),
+            (meta_out, meta_in, meta_send, meta_recv),
+        ):
+            copy = pltpu.make_async_remote_copy(
+                src_ref=src.at[o - 1],
+                dst_ref=dst.at[o - 1],
+                send_sem=send_sem.at[o - 1],
+                recv_sem=recv_sem.at[o - 1],
+                device_id={"ep": ahead[o]},
+            )
+            copy.start()
+            copies.append(copy)
+    for k in range(per):
+        arrived_ref[k] = cache_ref[chosen[0][k]]
+    meta_ref[0] = describe(0)
+    for copy in copies:
+        copy.wait_recv()
+    for o in range(1, SPAN):
+        for k in range(per):
+            arrived_ref[o * per + k] = cache_in[o - 1, k]
+        meta_ref[o] = meta_in[o - 1]
+    for copy in copies:
+        copy.wait_send()
+
+
+def migrate(kv_cache, cache_length, dest_device, dest_slot):
+    peers = lax.axis_size("ep")
+    per = kv_cache.shape[0] // SPAN
+    piece = pltpu.VMEM((SPAN - 1, per) + kv_cache.shape[1:], kv_cache.dtype)
+    note = pltpu.VMEM((SPAN - 1, 8, 128), jnp.int32)
+    smem = pl.BlockSpec(memory_space=pltpu.SMEM)
+    vmem = pl.BlockSpec(memory_space=pltpu.VMEM)
+    arrived, meta = pl.pallas_call(
+        functools.partial(migrate_kernel, peers),
+        out_shape=(
+            jax.ShapeDtypeStruct(kv_cache.shape, kv_cache.dtype),
+            jax.ShapeDtypeStruct((SPAN, 8, 128), jnp.int32),
+        ),
+        in_specs=[smem, smem, smem, vmem],
+        out_specs=(vmem, vmem),
+        scratch_shapes=[piece, piece, note, note]
+        + [pltpu.SemaphoreType.DMA((SPAN - 1,))] * 4,
+        compiler_params=pltpu.CompilerParams(
+            collective_id=1, has_side_effects=True, vmem_limit_bytes=16 * 1024 * 1024
+        ),
+    )(dest_device, dest_slot, cache_length, kv_cache)
+    return arrived, meta[:, 0, :per], meta[:, 0, per : 2 * per]
 
 
 def apply_rows(selector, values):
@@ -398,29 +488,11 @@
 ):
     device_count = lax.axis_size("ep")
     owned_count = kv_cache.shape[0]
-    group_rows = owned_count // SPAN
-    sender = order_matrix(dest_device, device_count, owned_count, group_rows)
-    sender_int = sender.astype(jnp.int32)
-    sender_bf = sender.astype(jnp.bfloat16)
-    ordered = apply_rows(sender_bf, kv_cache.reshape(owned_count, -1)).reshape(SPAN, group_rows, -1)
-    slot_meta = (jnp.sum(sender_int * (dest_slot + 1)[None, :], axis=1) - 1).reshape(
-        SPAN, group_rows
-    )
-    length_meta = jnp.sum(sender_int * cache_length[None, :], axis=1).reshape(SPAN, group_rows)
+    incoming, arrived_slot, arrived_length = migrate(
+        kv_cache, cache_length, dest_device, dest_slot
+    )
+    incoming = incoming.reshape(owned_count, -1)
     slot_range = jnp.arange(owned_count, dtype=jnp.int32)[:, None]
-    cache_pieces = [ordered[0]]
-    slot_pieces = [slot_meta[0]]
-    length_pieces = [length_meta[0]]
-    for offset in range(1, SPAN):
-        got_cache, got_slot, got_length = from_behind(
-            (ordered[offset], slot_meta[offset], length_meta[offset]), "ep", offset
-        )
-        cache_pieces.append(got_cache)
-        slot_pieces.append(got_slot)
-        length_pieces.append(got_length)
-    incoming = jnp.concatenate(cache_pieces, axis=0)
-    arrived_slot = jnp.concatenate(slot_pieces, axis=0)
-    arrived_length = jnp.concatenate(length_pieces, axis=0)
     chooser = arrived_slot.reshape(1, owned_count) == slot_range
     moved_cache = apply_rows(chooser.astype(jnp.bfloat16), incoming).reshape(kv_cache.shape)
     moved_length = jnp.sum(

time: 79.8 us -> 71.1 us (0.89)
  starting transfers between devices: 13.2 us -> 0 us
  Pallas kernels: 47.6 us -> 59.5 us
  waiting for transfers between devices: 4.68 us -> 0 us
  other arithmetic: 6.09 us -> 1.48 us
  local copies, waits for them, and re-layouts: 4.45 us -> 6.33 us
    ppermute x9 -> x0, starting transfers between devices: 13.2 us -> none  [from_behind(): lax.ppermute(array, axis, [(i, (i + by) % peers) for i in range(peers)])]
    pallas_call x0 -> x1, Pallas kernels: none -> 12.9 us  [migrate(): pl.pallas_call(functools.partial(migrate_kernel, peers), out_shape=(jax.S...]
    ppermute x9 -> x0, waiting for transfers between devices: 4.68 us -> none  [from_behind(): lax.ppermute(array, axis, [(i, (i + by) % peers) for i in range(peers)])]
    unnamed x9 -> x21, local copies, waits for them, and re-layouts: 3.37 us -> 5.33 us
    pallas_call x1, Pallas kernels: 47.6 us -> 46.6 us  [expert_layer(): pl.pallas_call(functools.partial(expert_kernel, bits), out_shape=jax.Shap...]
    dot_general x1, matrix products: 0.28 us -> 1.11 us  [attend(): jnp.einsum('rgjd,rtgd->rgjt', queries, stored[:, :, 0], preferred_element...]
    reduce_sum x2 -> x0, other arithmetic: 0.82 us -> none  [the longest x1 0.8 us: shards(): jnp.sum(sender_int * cache_length[None, :], axis=1)]
  transfers between devices with their start and end apart: 9 -> 0, of which waited for: 2 -> 0; matrix products, arithmetic and copies ran while one was open for 7% -> 0% of each run, Pallas kernels for 0% -> 0%
where the time goes in v3:
time: 71.1 us; the launch traced here: 70.7 us
  Pallas kernels  59.5 us (84%)
  local copies, waits for them, and re-layouts  6.33 us (9%)
  matrix products  2.56 us (4%)
  other arithmetic  1.48 us (2%)
  between operations  0.84 us (1%)
    pallas_call x1, Pallas kernels, expert_layer(): pl.pallas_call(functools.partial(expert_kernel, bits), out_shape=jax.Shap...  46.6 us
    pallas_call x1, Pallas kernels, migrate(): pl.pallas_call(functools.partial(migrate_kernel, peers), out_shape=(jax.S...  12.9 us
    unnamed x21, local copies, waits for them, and re-layouts  5.33 us

profile of v3, /device:TPU:0, one launch (start us, length us, event | category | flops | bytes accessed | tf_op | source)
XLA Modules:
  0.0 70.7 jit_solution(5225536269089978308)
XLA Ops:
  0.6 0.9 %copy-done = bf16[8,32,512]{2,1,0:T(8,128)(2,1)S(1)} copy-done((bf16[8,32,512]{2,1,0:T(8,128)(2,1)S(1)}, bf16[8,32,512]{2,1,0:T(8,128)(2,1)}, u32[]{:S(2)}) %copy-start) | copy-done | bytes 262168
  1.6 0.7 copy-done.1
  2.2 0.7 copy-done.2
  2.9 0.7 copy-done.3
  3.6 12.9 %shard_map.148 = (bf16[8,32,512]{2,1,0:T(8,128)(2,1)S(1)}, s32[4,8,128]{2,1,0:T(8,128)S(1)}) custom-call(s32[8]{0:T(128)S(1)} %copy-done.1, s32[8]{0:T(128)S(1)} %copy-done.2, s32[8]{0:T(128)S(1)} %copy-done.3, bf16[8,32,512]{2,1,0:T(8,128)(2,1)S(1)} %copy-done), custom_call_target="tpu_custom_call" | custom-call | tf_op jit(solution)/shard_map/pallas_call | solution.py:453
  16.5 0.1 slice_reduce_fusion
  16.6 0.1 eq.28
  16.6 0.1 mul.55
  16.7 0.1 select_reduce_fusion.2
  16.8 0.1 iota_compare_fusion.2
  16.9 0.2 copy.36
  17.1 0.2 convolution_convert_fusion
  17.3 1.1 %select_reduce_fusion = (f32[8,2,16]{2,1,0:T(2,128)S(1)}, f32[8,2,32,16]{2,3,1,0:T(8,128)S(1)}) fusion(pred[8,32]{1,0:T(8,128)(4,1)S(1)} %iota_compare_fusion.2, bf16[8,2,16,128]{3,0,2,1:T(8,128)(2,1)} %bitcast.48, bf16[8,32,1,2,128]{4,0,3,2,1:T(8,128)(2,1)S(1)} %get-tuple-element.20), kind=kOutput, calls=%fused_computation.13 | convolution fusion | flops 2121472 | bytes 230656 | tf_op jit(solution)/shard_map/rgjd,rtgd->rgjt/dot_general | solution.py:27
  18.4 0.7 %slice_bitcast_fusion = (bf16[8,2,128,1]{2,0,1,3:T(8,128)(2,1)S(1)}, bf16[8,1,2,128]{3,0,2,1:T(8,128)(2,1)S(1)}) fusion(bf16[8,2,2,128]{3,0,2,1:T(8,128)(2,1)} %bitcast.47), kind=kLoop, calls=%fused_computation.35 | loop fusion | bytes 16384 | tf_op jit(solution)/shard_map/squeeze | solution.py:31
  19.1 1.0 %fusion.8 = f32[8,2,1,16]{3,2,1,0:T(1,128)S(1)} fusion(bf16[8,2,16,128]{3,0,2,1:T(8,128)(2,1)} %bitcast.49, bf16[8,2,128,1]{2,0,1,3:T(8,128)(2,1)S(1)} %get-tuple-element.30), kind=kOutput, calls=%fused_computation.22 | convolution fusion | flops 65536 | bytes 70656 | tf_op jit(solution)/shard_map/rgjd,rgd->rgj/dot_general | solution.py:31
  20.2 0.2 bitcast_reduce_fusion
  20.4 0.3 fusion
  20.7 0.2 multiply_reduce_fusion
  20.9 0.1 multiply_convert_fusion
  21.0 0.1 select_reduce_fusion.1
  21.2 0.6 pad_maximum_fusion.folded_ref
  21.8 46.6 %shard_map.149 = bf16[8,4096]{1,0:T(8,128)(2,1)} custom-call(bf16[2,16,1152]{2,1,0:T(8,128)(2,1)} %pad_maximum_fusion.folded_ref, bf16[1,4096,384]{2,1,0:T(8,128)(2,1)} %gate_hbm.1, bf16[1,4096,384]{2,1,0:T(8,128)(2,1)} %up_hbm.1, bf16[1,384,4096]{2,1,0:T(8,128)(2,1)} %down_hbm.1), custom_call_target="tpu_custom_call" | custom-call | tf_op jit(solution)/shard_map/pallas_call | solution.py:336
  68.4 0.8 %copy.30 = bf16[8,32,512]{2,1,0:T(8,128)(2,1)} copy(bf16[8,32,512]{2,0,1:T(8,128)(2,1)S(1)} %bitcast.42) | data formatting | bytes 524288
  69.2 1.5 %copy.58 = bf16[8,4096]{1,0:T(8,128)(2,1)} copy(bf16[8,4096]{1,0:T(8,128)(2,1)} %shard_map.149) | data formatting | bytes 131072
  (26 shorter events, 0.1 us)
Async XLA Ops:
  0.6 1.0 %copy-start = (bf16[8,32,512]{2,1,0:T(8,128)(2,1)S(1)}, bf16[8,32,512]{2,1,0:T(8,128)(2,1)}, u32[]{:S(2)}) copy-start(bf16[8,32,512]{2,1,0:T(8,128)(2,1)} %cache_ref.1) | copy-start | bytes 786436
  1.6 0.7 copy-start.1
  2.2 0.7 copy-start.2
  2.9 0.7 copy-start.3
  3.6 17.1 %copy-start.4 = (bf16[8,4096]{1,0:T(8,128)(2,1)S(1)}, bf16[8,4096]{1,0:T(8,128)(2,1)}, u32[]{:S(2)}) copy-start(bf16[8,4096]{1,0:T(8,128)(2,1)} %param.19) | copy-start | bytes 196612
  3.6 17.3 %copy-start.6 = (bf16[4096]{0:T(1024)(128)(2,1)S(1)}, bf16[4096]{0:T(1024)(128)(2,1)}, u32[]{:S(2)}) copy-start(bf16[4096]{0:T(1024)(128)(2,1)} %param.20) | copy-start | bytes 24580
  3.6 17.4 %copy-start.8 = (bf16[8,8]{1,0:T(8,128)(2,1)S(1)}, bf16[8,8]{1,0:T(8,128)(2,1)}, u32[]{:S(2)}) copy-start(bf16[8,8]{1,0:T(8,128)(2,1)} %param.22) | copy-start | bytes 388
  3.6 17.5 %copy-start.7 = (s32[8,8]{1,0:T(8,128)S(1)}, s32[8,8]{1,0:T(8,128)}, u32[]{:S(2)}) copy-start(s32[8,8]{1,0:T(8,128)} %param.21) | copy-start | bytes 772
  20.8 47.6 %copy-start.5 = (bf16[8,4096]{1,0:T(8,128)(2,1)}, bf16[8,4096]{1,0:T(8,128)(2,1)S(1)}, u32[]{:S(2)}) copy-start(bf16[8,4096]{1,0:T(8,128)(2,1)S(1)} %get-tuple-element.40) | copy-start | bytes 196612

commit v4 on v3

--- a/solution.py
+++ b/solution.py
@@ -181,20 +181,22 @@
     for c in (1, 2):
         held[c][0] = block[:, starts[c] : starts[c] + gather[c]]
 
-    steps = {}
-    for i in range(bits):
-        count = 1 << i
+    by_depth = sorted(range(chips), key=lambda p: (p.bit_count(), p))
+    hops = {}
+    for p in by_depth:
         for c in range(3):
-            if i > 0:
-                steps[c, i - 1].wait_recv()
-            steps[c, i] = send(
-                held[c].at[pl.ds(0, count)],
-                held[c].at[pl.ds(count, count)],
-                step_send.at[c * bits + i],
-                step_recv.at[c * bits + i],
-                far[orders[c][i]],
-            )
-            sent.append(steps[c, i])
+            if p > 0:
+                hops[c, p].wait_recv()
+            for i in range(p.bit_length(), bits):
+                to = p + (1 << i)
+                hops[c, to] = send(
+                    held[c].at[p],
+                    held[c].at[to],
+                    step_send.at[c * chips + to],
+                    step_recv.at[c * chips + to],
+                    far[orders[c][i]],
+                )
+                sent.append(hops[c, to])
     loads[0].wait()
     loads[1].wait()
 
@@ -221,7 +223,6 @@
     swaps = []
     share = None
     for c in range(3):
-        steps[c, bits - 1].wait_recv()
         swap = send(held[c], other[c], pair_send.at[1 + c], pair_recv.at[1 + c], mate)
         swaps.append(swap)
         sent.append(swap)
@@ -258,42 +259,45 @@
         trade = send(given[c], taken[c], pair_send.at[4 + c], pair_recv.at[4 + c], mate)
         trades.append(trade)
         sent.append(trade)
-    base_sem = 3 * bits
+    base_sem = 3 * chips
     backs = {}
 
-    def back(c, i):
-        count = 1 << i
-        backs[c, i] = send(
-            total[c].at[pl.ds(count, count)],
-            landed[c].at[pl.ds(count, count)],
-            step_send.at[base_sem + c * bits + i],
-            step_recv.at[base_sem + c * bits + i],
+    def back(c, p):
+        i = p.bit_length() - 1
+        backs[c, p] = send(
+            total[c].at[p],
+            landed[c].at[p],
+            step_send.at[base_sem + c * chips + p],
+            step_recv.at[base_sem + c * chips + p],
             far[orders[c][i]],
         )
-        sent.append(backs[c, i])
+        sent.append(backs[c, p])
+
+    def block_of(p, values, c):
+        r = relative(orders[c], p)
+        return values[16 * r : 16 * r + 16] + taken[c][p].astype(jnp.float32)
 
     for c in range(3):
         value = down(c, core)
         trades[c].wait_recv()
-        for p in reversed(range(chips)):
-            r = relative(orders[c], p)
-            total[c][p] = (
-                value[16 * r : 16 * r + 16] + taken[c][p].astype(jnp.float32)
-            ).astype(jnp.bfloat16)
-        back(c, bits - 1)
+        for p in reversed(by_depth):
+            total[c][p] = block_of(p, value, c).astype(jnp.bfloat16)
+            if p >= chips // 2:
+                back(c, p)
     ends = []
-    for i in reversed(range(bits)):
-        count = 1 << i
+    for p in reversed(by_depth):
+        if p >= chips // 2:
+            continue
         for c in range(3):
-            backs[c, i].wait_recv()
-            value = total[c][0:count].astype(jnp.float32) + landed[c][
-                count : 2 * count
-            ].astype(jnp.float32)
-            if i > 0:
-                total[c][0:count] = value.astype(jnp.bfloat16)
-                back(c, i - 1)
+            value = total[c][p].astype(jnp.float32)
+            for i in reversed(range(p.bit_length(), bits)):
+                backs[c, p + (1 << i)].wait_recv()
+                value = value + landed[c][p + (1 << i)].astype(jnp.float32)
+            if p > 0:
+                total[c][p] = value.astype(jnp.bfloat16)
+                back(c, p)
             else:
-                ends.append(value[0])
+                ends.append(value)
     done = jnp.concatenate(ends, axis=1)
     rows = done.shape[0] // 2
     keep = jnp.where(core == 0, done[:rows], done[rows:])
@@ -355,8 +359,8 @@
             pltpu.SemaphoreType.DMA((3,)),
             pltpu.SemaphoreType.DMA((8,)),
             pltpu.SemaphoreType.DMA((8,)),
-            pltpu.SemaphoreType.DMA((6 * bits,)),
-            pltpu.SemaphoreType.DMA((6 * bits,)),
+            pltpu.SemaphoreType.DMA((6 * chips,)),
+            pltpu.SemaphoreType.DMA((6 * chips,)),
         ],
         compiler_params=pltpu.CompilerParams(
             collective_id=0, has_side_effects=True, vmem_limit_bytes=56 * 1024 * 1024

time: 71.1 us -> 62.7 us (0.88)
  Pallas kernels: 59.5 us -> 51.1 us
    pallas_call x1, Pallas kernels: 46.6 us -> 38.2 us  [expert_layer(): pl.pallas_call(functools.partial(expert_kernel, bits), out_shape=jax.Shap...]
where the time goes in v4:
time: 62.7 us; the launch traced here: 62.3 us
  Pallas kernels  51.1 us (81%)
  local copies, waits for them, and re-layouts  6.33 us (10%)
  matrix products  2.56 us (4%)
  other arithmetic  1.48 us (2%)
  between operations  0.84 us (1%)
    pallas_call x1, Pallas kernels, expert_layer(): pl.pallas_call(functools.partial(expert_kernel, bits), out_shape=jax.Shap...  38.2 us
    pallas_call x1, Pallas kernels, migrate(): pl.pallas_call(functools.partial(migrate_kernel, peers), out_shape=(jax.S...  12.9 us
    unnamed x21, local copies, waits for them, and re-layouts  5.33 us

profile of v4, /device:TPU:0, one launch (start us, length us, event | category | flops | bytes accessed | tf_op | source)
XLA Modules:
  0.0 62.3 jit_solution(10489465076014664034)
XLA Ops:
  0.6 0.9 %copy-done = bf16[8,32,512]{2,1,0:T(8,128)(2,1)S(1)} copy-done((bf16[8,32,512]{2,1,0:T(8,128)(2,1)S(1)}, bf16[8,32,512]{2,1,0:T(8,128)(2,1)}, u32[]{:S(2)}) %copy-start) | copy-done | bytes 262168
  1.6 0.7 %copy-done.1 = s32[8]{0:T(128)S(1)} copy-done((s32[8]{0:T(128)S(1)}, s32[8]{0:T(128)}, u32[]{:S(2)}) %copy-start.1) | copy-done | bytes 56
  2.2 0.7 %copy-done.2 = s32[8]{0:T(128)S(1)} copy-done((s32[8]{0:T(128)S(1)}, s32[8]{0:T(128)}, u32[]{:S(2)}) %copy-start.2) | copy-done | bytes 56
  2.9 0.7 %copy-done.3 = s32[8]{0:T(128)S(1)} copy-done((s32[8]{0:T(128)S(1)}, s32[8]{0:T(128)}, u32[]{:S(2)}) %copy-start.3) | copy-done | bytes 56
  3.6 12.9 %shard_map.148 = (bf16[8,32,512]{2,1,0:T(8,128)(2,1)S(1)}, s32[4,8,128]{2,1,0:T(8,128)S(1)}) custom-call(s32[8]{0:T(128)S(1)} %copy-done.1, s32[8]{0:T(128)S(1)} %copy-done.2, s32[8]{0:T(128)S(1)} %copy-done.3, bf16[8,32,512]{2,1,0:T(8,128)(2,1)S(1)} %copy-done), custom_call_target="tpu_custom_call" | custom-call | tf_op jit(solution)/shard_map/pallas_call | solution.py:457
  16.5 0.1 slice_reduce_fusion
  16.6 0.1 eq.28
  16.6 0.1 mul.55
  16.7 0.1 select_reduce_fusion.2
  16.8 0.1 iota_compare_fusion.2
  16.9 0.2 copy.36
  17.1 0.2 convolution_convert_fusion
  17.3 1.1 %select_reduce_fusion = (f32[8,2,16]{2,1,0:T(2,128)S(1)}, f32[8,2,32,16]{2,3,1,0:T(8,128)S(1)}) fusion(pred[8,32]{1,0:T(8,128)(4,1)S(1)} %iota_compare_fusion.2, bf16[8,2,16,128]{3,0,2,1:T(8,128)(2,1)} %bitcast.48, bf16[8,32,1,2,128]{4,0,3,2,1:T(8,128)(2,1)S(1)} %get-tuple-element.20), kind=kOutput, calls=%fused_computation.13 | convolution fusion | flops 2121472 | bytes 230656 | tf_op jit(solution)/shard_map/rgjd,rtgd->rgjt/dot_general | solution.py:27
  18.4 0.7 %slice_bitcast_fusion = (bf16[8,2,128,1]{2,0,1,3:T(8,128)(2,1)S(1)}, bf16[8,1,2,128]{3,0,2,1:T(8,128)(2,1)S(1)}) fusion(bf16[8,2,2,128]{3,0,2,1:T(8,128)(2,1)} %bitcast.47), kind=kLoop, calls=%fused_computation.35 | loop fusion | bytes 16384 | tf_op jit(solution)/shard_map/squeeze | solution.py:31
  19.1 1.0 %fusion.8 = f32[8,2,1,16]{3,2,1,0:T(1,128)S(1)} fusion(bf16[8,2,16,128]{3,0,2,1:T(8,128)(2,1)} %bitcast.49, bf16[8,2,128,1]{2,0,1,3:T(8,128)(2,1)S(1)} %get-tuple-element.30), kind=kOutput, calls=%fused_computation.22 | convolution fusion | flops 65536 | bytes 70656 | tf_op jit(solution)/shard_map/rgjd,rgd->rgj/dot_general | solution.py:31
  20.2 0.2 bitcast_reduce_fusion
  20.4 0.3 fusion
  20.7 0.2 multiply_reduce_fusion
  20.9 0.1 multiply_convert_fusion
  21.0 0.1 select_reduce_fusion.1
  21.2 0.6 %pad_maximum_fusion.folded_ref = bf16[2,16,1152]{2,1,0:T(8,128)(2,1)} fusion(bf16[1,16,1152]{2,1,0:T(8,128)(2,1)S(1)} %get-tuple-element.35, bf16[1,16,1152]{2,1,0:T(8,128)(2,1)S(1)} %get-tuple-element.34), kind=kLoop, calls=%fused_computation.15 | loop fusion | flops 36864 | bytes 147456 | tf_op jit(solution)/shard_map/stack | solution.py:327
  21.8 38.2 %shard_map.149 = bf16[8,4096]{1,0:T(8,128)(2,1)} custom-call(bf16[2,16,1152]{2,1,0:T(8,128)(2,1)} %pad_maximum_fusion.folded_ref, bf16[1,4096,384]{2,1,0:T(8,128)(2,1)} %gate_hbm.1, bf16[1,4096,384]{2,1,0:T(8,128)(2,1)} %up_hbm.1, bf16[1,384,4096]{2,1,0:T(8,128)(2,1)} %down_hbm.1), custom_call_target="tpu_custom_call" | custom-call | tf_op jit(solution)/shard_map/pallas_call | solution.py:340
  60.0 0.8 %copy.30 = bf16[8,32,512]{2,1,0:T(8,128)(2,1)} copy(bf16[8,32,512]{2,0,1:T(8,128)(2,1)S(1)} %bitcast.42) | data formatting | bytes 524288
  60.8 1.5 %copy.58 = bf16[8,4096]{1,0:T(8,128)(2,1)} copy(bf16[8,4096]{1,0:T(8,128)(2,1)} %shard_map.149) | data formatting | bytes 131072
  (26 shorter events, 0.1 us)
Async XLA Ops:
  0.6 1.0 %copy-start = (bf16[8,32,512]{2,1,0:T(8,128)(2,1)S(1)}, bf16[8,32,512]{2,1,0:T(8,128)(2,1)}, u32[]{:S(2)}) copy-start(bf16[8,32,512]{2,1,0:T(8,128)(2,1)} %cache_ref.1) | copy-start | bytes 786436
  1.6 0.7 %copy-start.1 = (s32[8]{0:T(128)S(1)}, s32[8]{0:T(128)}, u32[]{:S(2)}) copy-start(s32[8]{0:T(128)} %dest_ref.1) | copy-start | bytes 100
  2.2 0.7 %copy-start.2 = (s32[8]{0:T(128)S(1)}, s32[8]{0:T(128)}, u32[]{:S(2)}) copy-start(s32[8]{0:T(128)} %slot_ref.1) | copy-start | bytes 100
  2.9 0.7 %copy-start.3 = (s32[8]{0:T(128)S(1)}, s32[8]{0:T(128)}, u32[]{:S(2)}) copy-start(s32[8]{0:T(128)} %length_ref.1) | copy-start | bytes 100
  3.6 17.1 %copy-start.4 = (bf16[8,4096]{1,0:T(8,128)(2,1)S(1)}, bf16[8,4096]{1,0:T(8,128)(2,1)}, u32[]{:S(2)}) copy-start(bf16[8,4096]{1,0:T(8,128)(2,1)} %param.19) | copy-start | bytes 196612
  3.6 17.3 %copy-start.6 = (bf16[4096]{0:T(1024)(128)(2,1)S(1)}, bf16[4096]{0:T(1024)(128)(2,1)}, u32[]{:S(2)}) copy-start(bf16[4096]{0:T(1024)(128)(2,1)} %param.20) | copy-start | bytes 24580
  3.6 17.4 %copy-start.8 = (bf16[8,8]{1,0:T(8,128)(2,1)S(1)}, bf16[8,8]{1,0:T(8,128)(2,1)}, u32[]{:S(2)}) copy-start(bf16[8,8]{1,0:T(8,128)(2,1)} %param.22) | copy-start | bytes 388
  3.6 17.5 %copy-start.7 = (s32[8,8]{1,0:T(8,128)S(1)}, s32[8,8]{1,0:T(8,128)}, u32[]{:S(2)}) copy-start(s32[8,8]{1,0:T(8,128)} %param.21) | copy-start | bytes 772
  20.8 39.1 %copy-start.5 = (bf16[8,4096]{1,0:T(8,128)(2,1)}, bf16[8,4096]{1,0:T(8,128)(2,1)S(1)}, u32[]{:S(2)}) copy-start(bf16[8,4096]{1,0:T(8,128)(2,1)S(1)} %get-tuple-element.40) | copy-start | bytes 196612

commit v5 on v4

--- a/solution.py
+++ b/solution.py
@@ -370,9 +370,9 @@
 
 def migrate_kernel(
     peers,
-    dest_ref,
-    slot_ref,
-    length_ref,
+    dest_hbm,
+    slot_hbm,
+    length_hbm,
     cache_ref,
     arrived_ref,
     meta_ref,
@@ -384,7 +384,18 @@
     cache_recv,
     meta_send,
     meta_recv,
+    dest_ref,
+    slot_ref,
+    length_ref,
+    load_sem,
 ):
+    loads = []
+    for n, (src, dst) in enumerate(
+        ((dest_hbm, dest_ref), (slot_hbm, slot_ref), (length_hbm, length_ref))
+    ):
+        load = pltpu.make_async_copy(src, dst, load_sem.at[n])
+        load.start()
+        loads.append(load)
     me = lax.axis_index("ep")
     owned = cache_ref.shape[0]
     per = owned // SPAN
@@ -395,6 +406,8 @@
         pl.semaphore_signal(barrier, inc=1, device_id={"ep": ahead[o]})
         pl.semaphore_signal(barrier, inc=1, device_id={"ep": behind[o]})
 
+    for load in loads:
+        load.wait()
     counts = [jnp.int32(0)] * SPAN
     chosen = [[jnp.int32(0)] * per for _ in range(SPAN)]
     for i in range(owned):
@@ -452,7 +465,8 @@
     per = kv_cache.shape[0] // SPAN
     piece = pltpu.VMEM((SPAN - 1, per) + kv_cache.shape[1:], kv_cache.dtype)
     note = pltpu.VMEM((SPAN - 1, 8, 128), jnp.int32)
-    smem = pl.BlockSpec(memory_space=pltpu.SMEM)
+    hbm = pl.BlockSpec(memory_space=pl.ANY)
+    index = pltpu.SMEM((kv_cache.shape[0],), jnp.int32)
     vmem = pl.BlockSpec(memory_space=pltpu.VMEM)
     arrived, meta = pl.pallas_call(
         functools.partial(migrate_kernel, peers),
@@ -460,10 +474,12 @@
             jax.ShapeDtypeStruct(kv_cache.shape, kv_cache.dtype),
             jax.ShapeDtypeStruct((SPAN, 8, 128), jnp.int32),
         ),
-        in_specs=[smem, smem, smem, vmem],
+        in_specs=[hbm, hbm, hbm, vmem],
         out_specs=(vmem, vmem),
         scratch_shapes=[piece, piece, note, note]
-        + [pltpu.SemaphoreType.DMA((SPAN - 1,))] * 4,
+        + [pltpu.SemaphoreType.DMA((SPAN - 1,))] * 4
+        + [index] * 3
+        + [pltpu.SemaphoreType.DMA((3,))],
         compiler_params=pltpu.CompilerParams(
             collective_id=1, has_side_effects=True, vmem_limit_bytes=16 * 1024 * 1024
         ),

time: 62.7 us -> 62.2 us (level)
  no operation moved by 1% of the time
where the time goes in v5:
time: 62.2 us; the launch traced here: 61.7 us
  Pallas kernels  50.5 us (81%)
  local copies, waits for them, and re-layouts  6.33 us (10%)
  matrix products  2.56 us (4%)
  other arithmetic  1.48 us (2%)
  between operations  0.84 us (1%)
    pallas_call x1, Pallas kernels, expert_layer(): pl.pallas_call(functools.partial(expert_kernel, bits), out_shape=jax.Shap...  38.2 us
    pallas_call x1, Pallas kernels, migrate(): pl.pallas_call(functools.partial(migrate_kernel, peers), out_shape=(jax.S...  12.4 us
    unnamed x21, local copies, waits for them, and re-layouts  5.33 us

profile of v5, /device:TPU:0, one launch (start us, length us, event | category | flops | bytes accessed | tf_op | source)
XLA Modules:
  0.0 61.7 jit_solution(15034631913725507647)
XLA Ops:
  0.6 0.9 %copy-done = bf16[8,32,512]{2,1,0:T(8,128)(2,1)S(1)} copy-done((bf16[8,32,512]{2,1,0:T(8,128)(2,1)S(1)}, bf16[8,32,512]{2,1,0:T(8,128)(2,1)}, u32[]{:S(2)}) %copy-start) | copy-done | bytes 262168
  1.6 0.7 %copy-done.1 = s32[8]{0:T(128)S(1)} copy-done((s32[8]{0:T(128)S(1)}, s32[8]{0:T(128)}, u32[]{:S(2)}) %copy-start.1) | copy-done | bytes 56
  2.2 0.7 %copy-done.2 = s32[8]{0:T(128)S(1)} copy-done((s32[8]{0:T(128)S(1)}, s32[8]{0:T(128)}, u32[]{:S(2)}) %copy-start.2) | copy-done | bytes 56
  2.9 0.7 %copy-done.3 = s32[8]{0:T(128)S(1)} copy-done((s32[8]{0:T(128)S(1)}, s32[8]{0:T(128)}, u32[]{:S(2)}) %copy-start.3) | copy-done | bytes 56
  3.6 12.4 %shard_map.148 = (bf16[8,32,512]{2,1,0:T(8,128)(2,1)S(1)}, s32[4,8,128]{2,1,0:T(8,128)S(1)}) custom-call(s32[8]{0:T(128)S(1)} %copy-done.1, s32[8]{0:T(128)S(1)} %copy-done.2, s32[8]{0:T(128)S(1)} %copy-done.3, bf16[8,32,512]{2,1,0:T(8,128)(2,1)S(1)} %copy-done), custom_call_target="tpu_custom_call" | custom-call | tf_op jit(solution)/shard_map/pallas_call | solution.py:471
  16.0 0.1 slice_reduce_fusion
  16.0 0.1 eq.28
  16.1 0.1 mul.55
  16.2 0.1 select_reduce_fusion.2
  16.3 0.1 iota_compare_fusion.2
  16.4 0.2 copy.36
  16.6 0.2 convolution_convert_fusion
  16.8 1.1 %select_reduce_fusion = (f32[8,2,16]{2,1,0:T(2,128)S(1)}, f32[8,2,32,16]{2,3,1,0:T(8,128)S(1)}) fusion(pred[8,32]{1,0:T(8,128)(4,1)S(1)} %iota_compare_fusion.2, bf16[8,2,16,128]{3,0,2,1:T(8,128)(2,1)} %bitcast.48, bf16[8,32,1,2,128]{4,0,3,2,1:T(8,128)(2,1)S(1)} %get-tuple-element.20), kind=kOutput, calls=%fused_computation.13 | convolution fusion | flops 2121472 | bytes 230656 | tf_op jit(solution)/shard_map/rgjd,rtgd->rgjt/dot_general | solution.py:27
  17.9 0.7 %slice_bitcast_fusion = (bf16[8,2,128,1]{2,0,1,3:T(8,128)(2,1)S(1)}, bf16[8,1,2,128]{3,0,2,1:T(8,128)(2,1)S(1)}) fusion(bf16[8,2,2,128]{3,0,2,1:T(8,128)(2,1)} %bitcast.47), kind=kLoop, calls=%fused_computation.35 | loop fusion | bytes 16384 | tf_op jit(solution)/shard_map/squeeze | solution.py:31
  18.6 1.0 %fusion.8 = f32[8,2,1,16]{3,2,1,0:T(1,128)S(1)} fusion(bf16[8,2,16,128]{3,0,2,1:T(8,128)(2,1)} %bitcast.49, bf16[8,2,128,1]{2,0,1,3:T(8,128)(2,1)S(1)} %get-tuple-element.30), kind=kOutput, calls=%fused_computation.22 | convolution fusion | flops 65536 | bytes 70656 | tf_op jit(solution)/shard_map/rgjd,rgd->rgj/dot_general | solution.py:31
  19.6 0.2 bitcast_reduce_fusion
  19.9 0.3 fusion
  20.2 0.2 multiply_reduce_fusion
  20.4 0.1 multiply_convert_fusion
  20.5 0.1 select_reduce_fusion.1
  20.7 0.6 %pad_maximum_fusion.folded_ref = bf16[2,16,1152]{2,1,0:T(8,128)(2,1)} fusion(bf16[1,16,1152]{2,1,0:T(8,128)(2,1)S(1)} %get-tuple-element.35, bf16[1,16,1152]{2,1,0:T(8,128)(2,1)S(1)} %get-tuple-element.34), kind=kLoop, calls=%fused_computation.15 | loop fusion | flops 36864 | bytes 147456 | tf_op jit(solution)/shard_map/stack | solution.py:327
  21.3 38.2 %shard_map.149 = bf16[8,4096]{1,0:T(8,128)(2,1)} custom-call(bf16[2,16,1152]{2,1,0:T(8,128)(2,1)} %pad_maximum_fusion.folded_ref, bf16[1,4096,384]{2,1,0:T(8,128)(2,1)} %gate_hbm.1, bf16[1,4096,384]{2,1,0:T(8,128)(2,1)} %up_hbm.1, bf16[1,384,4096]{2,1,0:T(8,128)(2,1)} %down_hbm.1), custom_call_target="tpu_custom_call" | custom-call | tf_op jit(solution)/shard_map/pallas_call | solution.py:340
  59.5 0.8 %copy.30 = bf16[8,32,512]{2,1,0:T(8,128)(2,1)} copy(bf16[8,32,512]{2,0,1:T(8,128)(2,1)S(1)} %bitcast.42) | data formatting | bytes 524288
  60.3 1.5 %copy.58 = bf16[8,4096]{1,0:T(8,128)(2,1)} copy(bf16[8,4096]{1,0:T(8,128)(2,1)} %shard_map.149) | data formatting | bytes 131072
  (26 shorter events, 0.1 us)
Async XLA Ops:
  0.6 1.0 %copy-start = (bf16[8,32,512]{2,1,0:T(8,128)(2,1)S(1)}, bf16[8,32,512]{2,1,0:T(8,128)(2,1)}, u32[]{:S(2)}) copy-start(bf16[8,32,512]{2,1,0:T(8,128)(2,1)} %cache_ref.1) | copy-start | bytes 786436
  1.6 0.7 %copy-start.1 = (s32[8]{0:T(128)S(1)}, s32[8]{0:T(128)}, u32[]{:S(2)}) copy-start(s32[8]{0:T(128)} %dest_hbm.1) | copy-start | bytes 100
  2.2 0.7 %copy-start.2 = (s32[8]{0:T(128)S(1)}, s32[8]{0:T(128)}, u32[]{:S(2)}) copy-start(s32[8]{0:T(128)} %slot_hbm.1) | copy-start | bytes 100
  2.9 0.7 %copy-start.3 = (s32[8]{0:T(128)S(1)}, s32[8]{0:T(128)}, u32[]{:S(2)}) copy-start(s32[8]{0:T(128)} %length_hbm.1) | copy-start | bytes 100
  3.6 16.6 %copy-start.4 = (bf16[8,4096]{1,0:T(8,128)(2,1)S(1)}, bf16[8,4096]{1,0:T(8,128)(2,1)}, u32[]{:S(2)}) copy-start(bf16[8,4096]{1,0:T(8,128)(2,1)} %param.19) | copy-start | bytes 196612
  3.6 16.8 %copy-start.6 = (bf16[4096]{0:T(1024)(128)(2,1)S(1)}, bf16[4096]{0:T(1024)(128)(2,1)}, u32[]{:S(2)}) copy-start(bf16[4096]{0:T(1024)(128)(2,1)} %param.20) | copy-start | bytes 24580
  3.6 16.9 %copy-start.8 = (bf16[8,8]{1,0:T(8,128)(2,1)S(1)}, bf16[8,8]{1,0:T(8,128)(2,1)}, u32[]{:S(2)}) copy-start(bf16[8,8]{1,0:T(8,128)(2,1)} %param.22) | copy-start | bytes 388
  3.6 16.9 %copy-start.7 = (s32[8,8]{1,0:T(8,128)S(1)}, s32[8,8]{1,0:T(8,128)}, u32[]{:S(2)}) copy-start(s32[8,8]{1,0:T(8,128)} %param.21) | copy-start | bytes 772
  20.3 39.1 %copy-start.5 = (bf16[8,4096]{1,0:T(8,128)(2,1)}, bf16[8,4096]{1,0:T(8,128)(2,1)S(1)}, u32[]{:S(2)}) copy-start(bf16[8,4096]{1,0:T(8,128)(2,1)S(1)} %get-tuple-element.40) | copy-start | bytes 196612
